TPU v7x, 512 devices: a whole 4x8x8 slice. The times are simulated.
512 devices in a mesh: row: 32 (over y_hi, z, core), col: 16 (over x, y_lo).
Axes of the slice: x: 4, y: 8 (y_hi: 2, y_lo: 4; y = y_hi * 4 + y_lo), z: 8, core: 2. Of those that a mesh axis runs over, the one named last changes fastest.
Arguments:
- left_features: bfloat16 [128, 128, 256], P('row', 'col'), may hold values from -6 to 6
- right_features: bfloat16 [128, 128, 256], P('col', 'row'), may hold values from -6 to 6
- flow_offsets: int32 [2, 128, 128], P(None, 'row'), may hold values from -64 to 63
- look_cotangent: bfloat16 [128, 128, 324], P('row', 'col'), may hold values from -6 to 6
- hidden_state: bfloat16 [128, 128, 128], P('row', 'col'), may hold values from -0.8984375 to 0.8984375
- context: bfloat16 [128, 128, 128], P('row', 'col'), may hold values from -6 to 6
- motion_weight: float32 [324, 256], replicated, may hold values from -0.3125 to 0.3125
- row_gates: bfloat16 [5, 512, 256], replicated, may hold values from -0.125 to 0.125
- row_candidate: bfloat16 [5, 512, 128], replicated, may hold values from -0.125 to 0.125
- column_gates: bfloat16 [5, 512, 256], replicated, may hold values from -0.125 to 0.125
- column_candidate: bfloat16 [5, 512, 128], replicated, may hold values from -0.125 to 0.125
Outputs:
- new_hidden: float32 [128, 128, 128], P('row', 'col')
- grad_left: float32 [128, 128, 256], P('row', 'col')
- grad_right: float32 [128, 128, 256], P('col', 'row')
All inputs are finite; a program needn't handle non-finite values.
Results may differ from a plain program's by a relative error of at most 0.0029.
Values may be sent and summed in bfloat16 or wider, within the bound.
No kernel may reach another device: no remote copies, remote signals or barrier semaphores. Data moves between devices by JAX's collectives and lax.ppermute only.
A program may use at most 64 MiB of HBM per device.

v0:
```python
import jax
import jax.numpy as jnp
from jax import lax
from jax.sharding import PartitionSpec as P

LEVELS = 4
RADIUS = 4


def with_halo(cells, sides, width):
    for axis, dim in sides:
        count = lax.axis_size(axis)
        ends = count - 1
        head = lax.slice_in_dim(cells, 0, width, axis=dim)
        tail = lax.slice_in_dim(cells, cells.shape[dim] - width, cells.shape[dim], axis=dim)
        cells = jnp.concatenate(
            [
                lax.ppermute(tail, axis, [(i, (i + 1) % count) for i in range(ends)]),
                cells,
                lax.ppermute(head, axis, [((i + 1) % count, i) for i in range(ends)]),
            ],
            axis=dim,
        )
    return cells


def bands(center, factor, first, count):
    offsets = jnp.arange(2 * RADIUS + 1, dtype=jnp.int32) - RADIUS
    where_at = (jnp.floor_divide(center, factor) - first)[:, None] + offsets[None, :]
    cells = jnp.arange(count, dtype=jnp.int32)
    return (where_at[:, :, None] == cells[None, None, :]).astype(jnp.float32)


def window_block(
    volume_rows, cotangent_rows, center_row, center_col, first_row, rows_here, cols_here
):
    pixel_count = volume_rows.shape[0]
    window_side = 2 * RADIUS + 1
    window_area = window_side * window_side
    highest = lax.Precision.HIGHEST
    current = volume_rows.reshape(pixel_count, rows_here, cols_here)
    summed = jnp.zeros((pixel_count, rows_here, cols_here), jnp.float32)
    found_list = []
    for level_index in range(LEVELS):
        factor = 2**level_index
        level_rows = rows_here // factor
        level_cols = cols_here // factor
        if level_index > 0:
            shape_now = current.shape
            current = current.reshape(pixel_count, shape_now[1] // 2, 2, shape_now[2] // 2, 2).mean(
                axis=(2, 4)
            )
        row_band = bands(center_row, factor, first_row // factor, level_rows)
        col_band = bands(center_col, factor, 0, level_cols)
        inner = jnp.einsum("prc,pbc->prb", current, col_band, precision=highest)
        picked = jnp.einsum("par,prb->pab", row_band, inner, precision=highest)
        found_list.append(picked.reshape(pixel_count, window_area))
        cot_level = cotangent_rows[
            :, level_index * window_area : (level_index + 1) * window_area
        ].astype(jnp.float32)
        cot_level = cot_level.reshape(pixel_count, window_side, window_side)
        partial_rows = jnp.einsum("par,pab->prb", row_band, cot_level, precision=highest)
        level_grid = jnp.einsum("prb,pbc->prc", partial_rows, col_band, precision=highest) / (
            factor * factor
        )
        expanded = jnp.broadcast_to(
            level_grid.reshape(pixel_count, level_rows, 1, level_cols, 1),
            (pixel_count, level_rows, factor, level_cols, factor),
        )
        summed = summed + expanded.reshape(pixel_count, rows_here, cols_here)
    looked_rows = jnp.concatenate(found_list, axis=1)
    return (looked_rows, summed.reshape(pixel_count, rows_here * cols_here).astype(jnp.bfloat16))


def taps(source, weight, axis_index, length):
    summed = None
    for tap_index in range(weight.shape[0]):
        window_slice = lax.slice_in_dim(source, tap_index, tap_index + length, axis=axis_index)
        product = jnp.einsum(
            "abi,io->abo", window_slice, weight[tap_index], preferred_element_type=jnp.float32
        )
        summed = product if summed is None else summed + product
    return summed


def gru_pass(prior_state, inputs, gates_weight, candidate_weight, axis_index, length):
    hidden_size = prior_state.shape[-1]
    joined = jnp.concatenate([prior_state, inputs], axis=-1)
    gate_pair = jax.nn.sigmoid(taps(joined, gates_weight, axis_index, length + 4))
    update = gate_pair[..., :hidden_size]
    reset_gate = gate_pair[..., hidden_size:]
    inner_state = lax.slice_in_dim(prior_state, 2, length + 6, axis=axis_index).astype(jnp.float32)
    reset_state = (reset_gate * inner_state).astype(jnp.bfloat16)
    inner_inputs = lax.slice_in_dim(inputs, 2, length + 6, axis=axis_index)
    candidate = jnp.tanh(
        taps(
            jnp.concatenate([reset_state, inner_inputs], axis=-1),
            candidate_weight,
            axis_index,
            length,
        )
    )
    center_state = lax.slice_in_dim(prior_state, 4, length + 4, axis=axis_index).astype(jnp.float32)
    center_update = lax.slice_in_dim(update, 2, length + 2, axis=axis_index)
    return (1.0 - center_update) * center_state + center_update * candidate


def shards(
    left_features,
    right_features,
    flow_offsets,
    look_cotangent,
    hidden_state,
    context,
    motion_weight,
    row_gates,
    row_candidate,
    column_gates,
    column_candidate,
):
    left_block, cotangent_block = (
        lax.all_gather(left_features, "col", axis=1, tiled=True),
        lax.all_gather(look_cotangent, "col", axis=1, tiled=True),
    )
    right_stripe = lax.all_gather(right_features, "row", axis=1, tiled=True)
    rows_left, width, channels = left_block.shape
    rows_right = right_stripe.shape[0]
    factor = channels ** (-0.5)
    left_flat = left_block.reshape(rows_left * width, channels)
    right_flat = right_stripe.reshape(rows_right * width, channels)
    row_ids = lax.axis_index("row") * rows_left + jnp.arange(rows_left, dtype=jnp.int32)
    col_ids = jnp.arange(width, dtype=jnp.int32)
    center_row = row_ids[:, None] + flow_offsets[0]
    center_col = col_ids[None, :] + flow_offsets[1]
    first_row = lax.axis_index("col") * rows_right
    volume = (
        lax.dot_general(
            left_flat, right_flat, (((1,), (1,)), ((), ())), preferred_element_type=jnp.float32
        )
        * factor
    )
    volume_rows = volume.reshape(rows_left, width, rows_right * width)

    def one_image_row(pieces):
        volume_piece, cot_piece, row_piece, col_piece = pieces
        return window_block(
            volume_piece, cot_piece, row_piece, col_piece, first_row, rows_right, width
        )

    looked_rows, spread_rows = lax.map(
        one_image_row, (volume_rows, cotangent_block, center_row, center_col)
    )
    looked_part = looked_rows.reshape(rows_left * width, -1)
    spread = spread_rows.reshape(rows_left * width, rows_right * width)
    grad_left_part = (
        jnp.dot(spread, right_flat, preferred_element_type=jnp.float32) * factor
    ).reshape(rows_left, width, channels)
    grad_right_part = (
        lax.dot_general(
            spread, left_flat, (((0,), (0,)), ((), ())), preferred_element_type=jnp.float32
        )
        * factor
    )
    grad_right_part = grad_right_part.reshape(rows_right, width, channels)
    outgoing = looked_part.reshape(rows_left, width, -1)
    summed_part, grad_left = (
        lax.psum_scatter(outgoing, "col", scatter_dimension=1, tiled=True),
        lax.psum_scatter(grad_left_part, "col", scatter_dimension=1, tiled=True),
    )
    grad_right = lax.psum_scatter(grad_right_part, "row", scatter_dimension=1, tiled=True)
    tile_rows = summed_part.shape[0]
    tile_cols = summed_part.shape[1]
    motion = jax.nn.relu(
        jnp.dot(
            summed_part.reshape(tile_rows * tile_cols, -1),
            motion_weight,
            precision=lax.Precision.HIGHEST,
        )
    )
    motion = motion.reshape(tile_rows, tile_cols, -1)
    inputs = jnp.concatenate([motion.astype(jnp.bfloat16), context], axis=-1)
    wide_state, wide_inputs = (
        with_halo(hidden_state, (("row", 0), ("col", 1)), 4),
        with_halo(inputs, (("row", 0), ("col", 1)), 4),
    )
    middle_state = gru_pass(wide_state, wide_inputs, row_gates, row_candidate, 1, tile_cols).astype(
        jnp.bfloat16
    )
    middle_inputs = lax.slice_in_dim(wide_inputs, 4, tile_cols + 4, axis=1)
    new_hidden = gru_pass(middle_state, middle_inputs, column_gates, column_candidate, 0, tile_rows)
    return (new_hidden, grad_left, grad_right)


def solution(mesh):
    in_specs = (
        P("row", "col", None),
        P("col", "row", None),
        P(None, "row", None),
        P("row", "col", None),
        P("row", "col", None),
        P("row", "col", None),
        P(),
        P(),
        P(),
        P(),
        P(),
    )
    out_specs = (P("row", "col", None), P("row", "col", None), P("col", "row", None))
    return jax.shard_map(shards, mesh=mesh, in_specs=in_specs, out_specs=out_specs, check_vma=False)
```

profile of v0, /device:TPU:56, one launch (start us, length us, event | category | flops | bytes accessed | tf_op | source)
XLA Modules:
  0.0 536.6 jit_solution(6397000688218133585)
XLA Ops:
  7.3 36.9 %all_gather.9 = bf16[4,128,256]{2,1,0:T(8,128)(2,1)S(1)} all-gather(bf16[4,8,256]{2,1,0:T(8,128)(2,1)} %param.13), channel_id=1, replica_groups=mesh['row'=32,'col'=16] {'col'}, dimensions={1}, use_global_device_ids=true | all-gather | bytes 278528 | tf_op jit(solution)/shard_map/all_gather | solution.py:122
  44.9 56.7 %all_gather.10 = bf16[8,128,256]{2,0,1:T(8,128)(2,1)S(1)} all-gather(bf16[8,4,256]{2,0,1:T(8,128)(2,1)S(1)} %copy.146), channel_id=1, replica_groups=mesh['row'=32,'col'=16] {'row'}, dimensions={1}, use_global_device_ids=true | all-gather | bytes 540672 | tf_op jit(solution)/shard_map/all_gather | solution.py:125
  101.7 45.6 %all_gather.11 = bf16[4,128,324]{2,0,1:T(4,128)(2,1)S(1)} all-gather(bf16[4,8,324]{2,0,1:T(4,128)(2,1)S(1)} %copy.148), channel_id=1, replica_groups=mesh['row'=32,'col'=16] {'col'}, dimensions={1}, use_global_device_ids=true | all-gather | bytes 352512 | tf_op jit(solution)/shard_map/all_gather | solution.py:123
  148.3 1.8 convolution_multiply_fusion.1
  150.2 84.4 %while.15 = (s32[]{:T(128)}, f32[4,128,324]{1,2,0:T(8,128)}, bf16[4,128,1024]{2,1,0:T(8,128)(2,1)}, s32[4,128]{1,0:T(4,128)S(1)}, s32[]{:T(128)}, /*index=5*/f32...) while((s32[]{:T(128)}, f32[4,128,324]{1,2,0:T(8,128)}, ...), condition=%wide.region_5.6_spmd, body=%wide.region_0.5_spmd.sunk | while | flops 40958856 | bytes 14476237 | solution.py:150
  151.2 1.1 constant_dynamic-slice_fusion.4
  160.2 1.2 fusion.192
  181.3 1.2 fusion.192
  202.4 1.2 fusion.192
  223.5 1.2 fusion.192
  234.6 2.4 copy.151
  237.6 1.6 copy.153
  239.3 1.9 collective-permute-start
  241.2 9.7 %collective-permute-start.1 = (bf16[4,8,128]{2,1,0:T(8,128)(2,1)S(1)}, bf16[4,8,128]{2,1,0:T(8,128)(2,1)S(1)}, u32[]{:S(2)}, u32[]{:S(2)}) collective-permute-start(bf16[4,8,128]{2,1,0:T(8,128)(2,1)S(1)} %copy-done.14), channel_id=1, source_target_pairs={{16,0},{32,16},{48,32},{64,48},{80,64},{96,80},{112,96},{128,112},... | collective-permute-start | bytes 24584 | tf_op jit(solution)/shard_map/ppermute | solution.py:20
  250.9 1.3 collective-permute-done.1
  252.2 61.6 %reduce-scatter.4.cloned.1.call-done = f32[4,8,324]{2,1,0:T(8,128)} async-done(((f32[4,128,324]{2,1,0:T(8,128)}), f32[4,8,324]{2,1,0:T(8,128)}) %reduce-scatter.4.cloned.1.call-update) | async-done | bytes 41488 | tf_op jit(solution)/shard_map/reduce_scatter | solution.py:167
  314.9 1.9 collective-permute-start.5
  316.8 2.4 collective-permute-start.4
  319.3 4.7 collective-permute-start.3
  324.0 3.8 collective-permute-start.2
  328.0 4.7 collective-permute-start.7
  332.8 3.8 collective-permute-start.6
  336.6 1.3 convolution_multiply_fusion.2
  337.9 1.8 collective-permute-done.6
  339.9 1.2 fusion.67
  341.1 1.2 convolution_add_fusion.4
  342.2 1.2 convolution_add_fusion.3
  343.4 1.2 convolution_add_fusion.2
  344.6 1.2 fusion.40
  349.8 99.6 %reduce-scatter.8.cloned.1.call-done = f32[8,4,256]{2,0,1:T(8,128)} async-done(((f32[8,128,256]{2,0,1:T(8,128)}), f32[8,4,256]{2,0,1:T(8,128)}) %reduce-scatter.8.cloned.1.call-update) | async-done | bytes 32784 | tf_op jit(solution)/shard_map/reduce_scatter | solution.py:170
  449.4 1.4 copy.154
  450.8 79.3 %reduce-scatter.6.cloned.1.call-done = f32[4,8,256]{2,1,0:T(8,128)} async-done(((f32[4,128,256]{2,1,0:T(8,128)}), f32[4,8,256]{2,1,0:T(8,128)}) %reduce-scatter.6.cloned.1.call-update) | async-done | bytes 32784 | tf_op jit(solution)/shard_map/reduce_scatter | solution.py:168
  (402 shorter events, 84.8 us)
Async XLA Ops:
  7.2 306.6 %copy-start = (f32[324,256]{1,0:T(8,128)S(1)}, f32[324,256]{1,0:T(8,128)}, u32[]{:S(2)}) copy-start(f32[324,256]{1,0:T(8,128)} %param.19) | copy-start | bytes 995332
  7.2 94.5 %copy-start.11 = (bf16[4,8,324]{2,1,0:T(8,128)(2,1)S(1)}, bf16[4,8,324]{2,1,0:T(8,128)(2,1)}, u32[]{:S(2)}) copy-start(bf16[4,8,324]{2,1,0:T(8,128)(2,1)} %param.16) | copy-start | bytes 62212
  7.2 306.6 %reduce-scatter.4.cloned.1.call-start = ((), (), s32[]{:S(2)}) async-start(), calls=%async_computation.3 | async-start | bytes 835584 | tf_op jit(solution)/shard_map/reduce_scatter | solution.py:167
  44.1 104.2 %copy-start.2 = (bf16[4,128,256]{2,1,0:T(8,128)(2,1)}, bf16[4,128,256]{2,1,0:T(8,128)(2,1)S(1)}, u32[]{:S(2)}) copy-start(bf16[4,128,256]{2,1,0:T(8,128)(2,1)S(1)} %all_gather.9) | copy-start | bytes 786436
  44.9 103.4 %copy-start.15 = (s32[2,4,128]{2,1,0:T(4,128)S(1)}, s32[2,4,128]{2,1,0:T(4,128)}, u32[]{:S(2)}) copy-start(s32[2,4,128]{2,1,0:T(4,128)} %param.15) | copy-start | bytes 12292
  150.2 2.7 copy-start.12
  157.2 2.5 copy-start.4
  162.5 1.9 copy-start.7
  169.4 1.9 copy-start.13
  171.3 2.7 copy-start.12
  178.4 2.5 copy-start.4
  190.5 1.9 copy-start.13
  192.4 2.7 copy-start.12
  199.4 2.5 copy-start.4
  204.7 1.9 copy-start.7
  211.6 1.9 copy-start.13
  213.5 2.7 copy-start.12
  220.6 2.5 copy-start.4
  225.9 1.9 copy-start.7
  234.6 2.5 copy-start.1
  234.6 2.5 copy-start.3
  237.0 212.4 %reduce-scatter.8.cloned.1.call-start = ((), (), s32[]{:S(2)}) async-start(), calls=%async_computation.5 | async-start | bytes 1081344 | tf_op jit(solution)/shard_map/reduce_scatter | solution.py:170
  237.6 77.3 %copy-start.9 = (bf16[4,8,128]{2,1,0:T(8,128)(2,1)S(1)}, bf16[4,8,128]{2,1,0:T(8,128)(2,1)}, u32[]{:S(2)}) copy-start(bf16[4,8,128]{2,1,0:T(8,128)(2,1)} %param.18) | copy-start | bytes 24580
  239.2 290.9 %reduce-scatter.6.cloned.1.call-start = ((), (), s32[]{:S(2)}) async-start(), calls=%async_computation.4 | async-start | bytes 557056 | tf_op jit(solution)/shard_map/reduce_scatter | solution.py:168
  239.3 11.6 %collective-permute-start = (bf16[4,8,128]{2,1,0:T(8,128)(2,1)S(1)}, bf16[4,8,128]{2,1,0:T(8,128)(2,1)S(1)}, u32[]{:S(2)}, u32[]{:S(2)}) collective-permute-start(bf16[4,8,128]{2,1,0:T(8,128)(2,1)S(1)} %copy-done.14), channel_id=1, source_target_pairs={{0,16},{16,32},{32,48},{48,64},{64,80},{80,96},{96,112},{112,128},... | collective-permute-start | bytes 24584 | tf_op jit(solution)/shard_map/ppermute | solution.py:18
  241.2 11.0 %collective-permute-start.1 = (bf16[4,8,128]{2,1,0:T(8,128)(2,1)S(1)}, bf16[4,8,128]{2,1,0:T(8,128)(2,1)S(1)}, u32[]{:S(2)}, u32[]{:S(2)}) collective-permute-start(bf16[4,8,128]{2,1,0:T(8,128)(2,1)S(1)} %copy-done.14), channel_id=1, source_target_pairs={{16,0},{32,16},{48,32},{64,48},{80,64},{96,80},{112,96},{128,112},... | collective-permute-start | bytes 24584 | tf_op jit(solution)/shard_map/ppermute | solution.py:20
  314.9 12.9 %collective-permute-start.5 = (bf16[4,8,384]{2,1,0:T(8,128)(2,1)S(1)}, bf16[4,8,384]{2,1,0:T(8,128)(2,1)S(1)}, u32[]{:S(2)}, u32[]{:S(2)}) collective-permute-start(bf16[4,8,384]{2,1,0:T(8,128)(2,1)S(1)} %pad_maximum_fusion.9), channel_id=1, source_target_pairs={{16,0},{32,16},{48,32},{64,48},{80,64},{96,80},{112,96},{128,112},... | collective-permute-start | bytes 73736 | tf_op jit(solution)/shard_map/ppermute | solution.py:20
  316.8 11.2 %collective-permute-start.4 = (bf16[4,8,384]{2,1,0:T(8,128)(2,1)S(1)}, bf16[4,8,384]{2,1,0:T(8,128)(2,1)S(1)}, u32[]{:S(2)}, u32[]{:S(2)}) collective-permute-start(bf16[4,8,384]{2,1,0:T(8,128)(2,1)S(1)} %pad_maximum_fusion.9), channel_id=1, source_target_pairs={{0,16},{16,32},{32,48},{48,64},{64,80},{80,96},{96,112},{112,128},... | collective-permute-start | bytes 73736 | tf_op jit(solution)/shard_map/ppermute | solution.py:18
  319.3 18.7 %collective-permute-start.3 = (bf16[12,4,128]{2,1,0:T(4,128)(2,1)S(1)}, bf16[12,4,128]{2,1,0:T(4,128)(2,1)S(1)}, u32[]{:S(2)}, u32[]{:S(2)}) collective-permute-start(bf16[12,4,128]{2,1,0:T(4,128)(2,1)S(1)} %get-tuple-element.431), channel_id=1, source_target_pairs={{1,0},{2,1},{3,2},{4,3},{5,4},{6,5},{7,6},{8,7},{9,8},{10,9},{11,1... | collective-permute-start | bytes 36872 | tf_op jit(solution)/shard_map/ppermute | solution.py:20
  324.0 13.9 %collective-permute-start.2 = (bf16[12,4,128]{2,1,0:T(4,128)(2,1)S(1)}, bf16[12,4,128]{2,1,0:T(4,128)(2,1)S(1)}, u32[]{:S(2)}, u32[]{:S(2)}) collective-permute-start(bf16[12,4,128]{2,1,0:T(4,128)(2,1)S(1)} %get-tuple-element.430), channel_id=1, source_target_pairs={{0,1},{1,2},{2,3},{3,4},{4,5},{5,6},{6,7},{7,8},{8,9},{9,10},{10,1... | collective-permute-start | bytes 36872 | tf_op jit(solution)/shard_map/ppermute | solution.py:18
  328.0 9.9 %collective-permute-start.7 = (bf16[12,4,384]{2,1,0:T(4,128)(2,1)S(1)}, bf16[12,4,384]{2,1,0:T(4,128)(2,1)S(1)}, u32[]{:S(2)}, u32[]{:S(2)}) collective-permute-start(bf16[12,4,384]{2,1,0:T(4,128)(2,1)S(1)} %get-tuple-element.429), channel_id=1, source_target_pairs={{1,0},{2,1},{3,2},{4,3},{5,4},{6,5},{7,6},{8,7},{9,8},{10,9},{11,1... | collective-permute-start | bytes 110600 | tf_op jit(solution)/shard_map/ppermute | solution.py:20
  332.8 7.0 %collective-permute-start.6 = (bf16[12,4,384]{2,1,0:T(4,128)(2,1)S(1)}, bf16[12,4,384]{2,1,0:T(4,128)(2,1)S(1)}, u32[]{:S(2)}, u32[]{:S(2)}) collective-permute-start(bf16[12,4,384]{2,1,0:T(4,128)(2,1)S(1)} %get-tuple-element.428), channel_id=1, source_target_pairs={{0,1},{1,2},{2,3},{3,4},{4,5},{5,6},{6,7},{7,8},{8,9},{9,10},{10,1... | collective-permute-start | bytes 110600 | tf_op jit(solution)/shard_map/ppermute | solution.py:18
  (14 other events, 17.4 us)
Sparse Core Ops, SparseCore 0:
  237.1 76.6 reduce-scatter.3
  319.1 130.1 reduce-scatter.7
  452.7 77.2 reduce-scatter.5
where the time goes:
time: 545 us; the launch traced here: 537 us
  waiting for transfers between devices  244 us (45%)
  blocking collectives  139 us (26%)
  matrix products  55 us (10%)
  local copies, waits for them, and re-layouts  41 us (8%)
  starting transfers between devices  33.1 us (6%)
  between operations  14.2 us (3%)
  other arithmetic  8.71 us (2%)
    reduce_scatter x1, waiting for transfers between devices, shards(): lax.psum_scatter(grad_right_part, 'row', scatter_dimension=1, tiled=True)  99.6 us
    reduce_scatter x1, waiting for transfers between devices, shards(): lax.psum_scatter(grad_left_part, 'col', scatter_dimension=1, tiled=True)  79.3 us
    reduce_scatter x1, waiting for transfers between devices, shards(): lax.psum_scatter(outgoing, 'col', scatter_dimension=1, tiled=True)  61.6 us
    all_gather x1, blocking collectives, shards(): right_stripe = lax.all_gather(right_features, 'row', axis=1, tiled=True)  56.7 us
    all_gather x1, blocking collectives, shards(): lax.all_gather(look_cotangent, 'col', axis=1, tiled=True)  45.6 us
    all_gather x1, blocking collectives, shards(): lax.all_gather(left_features, 'col', axis=1, tiled=True)  36.9 us
    ppermute x4, starting transfers between devices, with_halo(): lax.ppermute(head, axis, [((i + 1) % count, i) for i in range(ends)])  21.1 us
    dot_general x12, matrix products, window_block(): inner = jnp.einsum('prc,pbc->prb', current, col_band, precision=highest)  12.9 us
  transfers between devices with their start and end apart: 11, of which 6 were waited for; matrix products, arithmetic and copies ran while one was open for 3% of the time, Pallas kernels for 0%

commit v1 on v0

v1 whole, which is shorter than its diff:
```python
import jax
import jax.numpy as jnp
import numpy as np
from jax import lax
from jax.experimental import pallas as pl
from jax.experimental.pallas import tpu as pltpu
from jax.sharding import PartitionSpec as P

LEVELS = 4
RADIUS = 4
SIDE = 2 * RADIUS + 1
AREA = SIDE * SIDE
LANES = 128
F32 = jnp.float32
BF16 = jnp.bfloat16
I32 = jnp.int32


def iota(shape, dim):
    return lax.broadcasted_iota(I32, shape, dim)


def target_of(row, strip, col):
    return ((row >> 3) << 6) | (strip << 5) | ((row & 7) << 2) | col


def pool_matrix(rows, strips, width):
    count = np.arange(rows * strips * width)
    strip, row, col = count // (rows * width), count // width % rows, count % width
    target = target_of(row, strip, col)
    parts = []
    for level in (1, 2, 3):
        high, wide = rows >> level, max(width >> level, 1)
        cell = (strip * high + (row >> level)) * wide + (col >> level)
        part = np.zeros((strips * high * wide, count.size), np.float32)
        part[cell, target] = 0.25**level
        parts.append(part)
    pooled = np.concatenate(parts, axis=0)
    padded = -(-pooled.shape[0] // LANES) * LANES
    return np.pad(pooled, ((0, padded - pooled.shape[0]), (0, 0))).astype(BF16)


def take(values, index):
    return jnp.take_along_axis(values, index & (LANES - 1), axis=1, mode="promise_in_bounds")


def inside(index, count):
    return (index >= 0) & (index < count)


def pack(cells, tile_cols, channels, lefts):
    width = channels + LEVELS * AREA + 2

    def kernel(left_ref, cot_ref, flow_ref, right_ref, lefts_hbm, right_out, left, wide, sems):
        first_col = lax.axis_index(COL) * tile_cols
        for row in range(right_ref.shape[0]):
            step = right_ref.shape[1]
            wide[row * step : (row + 1) * step, :] = right_ref[row].astype(F32)
        right_out[...] = wide[...].astype(BF16)
        left[:, :channels] = left_ref[...]
        left[:, channels : width - 2] = cot_ref[...]
        chosen = iota((tile_cols, LANES), 1) == first_col + iota((tile_cols, LANES), 0)
        for axis in range(2):
            columns = []
            for row in range(cells // tile_cols):
                values = jnp.broadcast_to(flow_ref[axis, row : row + 1, :].astype(F32), (tile_cols, LANES))
                columns.append(jnp.sum(jnp.where(chosen, values, 0.0), axis=1, keepdims=True))
            column = jnp.concatenate(columns, axis=0).astype(BF16)
            left[:, width - 2 + axis : width - 1 + axis] = column
        copies = [pltpu.make_async_copy(left, lefts_hbm.at[i], sems.at[i]) for i in range(lefts)]
        for copy in copies:
            copy.start()
        for copy in copies:
            copy.wait()

    vmem, hbm = pl.BlockSpec(memory_space=pltpu.VMEM), pl.BlockSpec(memory_space=pltpu.HBM)
    return pl.pallas_call(
        kernel,
        out_shape=(
            jax.ShapeDtypeStruct((lefts, cells, width), BF16),
            jax.ShapeDtypeStruct((cells, channels), BF16),
        ),
        in_specs=[vmem] * 4,
        out_specs=[hbm, vmem],
        scratch_shapes=[
            pltpu.VMEM((cells, width), BF16),
            pltpu.VMEM((cells, channels), F32),
            pltpu.SemaphoreType.DMA((lefts,)),
        ],
        compiler_params=pltpu.CompilerParams(vmem_limit_bytes=60 * 2**20),
        name="pack",
    )


def centers_of(place, given, index, chunk):
    shape = (chunk, LANES)
    pixel = index * chunk + iota(shape, 0)
    core = place[2] ^ (pixel >> 8)
    row = place[0] + ((pixel >> 5) & 7) * 8 + core * 4 + ((pixel >> 3) & 3)
    col = place[1] + (pixel & 7)
    row = row + jnp.broadcast_to(given[:, LEVELS * AREA : LEVELS * AREA + 1], shape).astype(I32)
    col = col + jnp.broadcast_to(given[:, LEVELS * AREA + 1 : LEVELS * AREA + 2], shape).astype(I32)
    return [(row >> level, col >> level) for level in range(LEVELS)]


def spread_out(pixels, channels, targets, chunk, blocks):
    tiles = targets // LANES
    size = targets // blocks
    half = pixels // 2

    def kernel(
        place, own_ref, other_ref, pool_ref, spread_hbm, grad_hbm,
        left, rest, fine, coarse, spread_ref, grad_ref, sems,
    ):
        scale = channels**-0.5
        first = place[3]
        left[:half, :] = own_ref[:, :channels]
        left[half:, :] = other_ref[:, :channels]
        rest[:half, :] = own_ref[:, channels:]
        rest[half:, :] = other_ref[:, channels:]

        def step(index, carry):
            rows = pl.ds(pl.multiple_of(index * chunk, chunk), chunk)
            shape = (chunk, LANES)
            lane = iota(shape, 1)
            given = rest[rows, :].astype(F32)
            centers = centers_of(place, given, index, chunk)
            cots = []
            for level in range(LEVELS):
                part = given[:, level * AREA : (level + 1) * AREA]
                cots.append(jnp.pad(part, ((0, 0), (0, LANES - AREA))))

            def window(level, row, col):
                a, b = row - centers[level][0], col + (first >> level) - centers[level][1]
                valid = (jnp.abs(a) <= RADIUS) & (jnp.abs(b) <= RADIUS)
                return jnp.where(valid, take(cots[level], a * SIDE + b + AREA // 2), 0.0)

            flip = place[4]
            a = ((lane >> 6) << 3) + ((lane >> 2) & 7) - centers[0][0]
            b = ((((lane >> 5) & 1) ^ flip) << 6) + (lane & 3) + first - centers[0][1]
            near_col = jnp.abs(b) <= RADIUS
            entry = a * SIDE + b + AREA // 2
            for tile in range(tiles):
                valid = near_col & (jnp.abs(a + 16 * tile) <= RADIUS)
                picked = take(cots[0], entry + 16 * SIDE * tile)
                fine[rows, tile * LANES : (tile + 1) * LANES] = jnp.where(valid, picked, 0.0)
            for tile in range(2):
                cell = window(1, lane >> 1, ((tile ^ flip) << 5) + (lane & 1))
                coarse[rows, tile * LANES : (tile + 1) * LANES] = cell.astype(BF16)
            second = window(2, lane & 31, (((lane >> 5) & 1) ^ flip) << 4)
            third = window(3, lane & 15, (((lane >> 4) & 1) ^ flip) << 3)
            cell = jnp.where(lane < 64, second, jnp.where(lane < 96, third, 0.0))
            coarse[rows, 2 * LANES :] = cell.astype(BF16)
            return carry

        lax.fori_loop(0, pixels // chunk, step, 0)

        spread = (fine[...] + jnp.dot(coarse[...], pool_ref[...], preferred_element_type=F32)).astype(BF16)
        spread_ref[...] = spread
        spread_copy = pltpu.make_async_copy(spread_ref, spread_hbm, sems.at[0])
        spread_copy.start()
        grad_ref[...] = (
            lax.dot_general(spread, left[...], (((0,), (0,)), ((), ())), preferred_element_type=F32) * scale
        ).astype(BF16)
        grad_copies = []
        for block in range(blocks):
            owner = ((block & 1) ^ place[4]) * (blocks // 2) + (block >> 1)
            copy = pltpu.make_async_copy(
                grad_ref.at[block * size : (block + 1) * size], grad_hbm.at[owner], sems.at[1 + block]
            )
            copy.start()
            grad_copies.append(copy)
        spread_copy.wait()
        for copy in grad_copies:
            copy.wait()

    vmem, hbm = pl.BlockSpec(memory_space=pltpu.VMEM), pl.BlockSpec(memory_space=pltpu.HBM)
    return pl.pallas_call(
        kernel,
        out_shape=(
            jax.ShapeDtypeStruct((pixels, targets), BF16),
            jax.ShapeDtypeStruct((blocks, size, channels), BF16),
        ),
        in_specs=[pl.BlockSpec(memory_space=pltpu.SMEM)] + [vmem] * 3,
        out_specs=[hbm] * 2,
        scratch_shapes=[
            pltpu.VMEM((pixels, channels), BF16),
            pltpu.VMEM((pixels, LEVELS * AREA + 2), BF16),
            pltpu.VMEM((pixels, targets), F32),
            pltpu.VMEM((pixels, 3 * LANES), BF16),
            pltpu.VMEM((pixels, targets), BF16),
            pltpu.VMEM((targets, channels), BF16),
            pltpu.SemaphoreType.DMA((1 + blocks,)),
        ],
        compiler_params=pltpu.CompilerParams(vmem_limit_bytes=24 * 2**20),
        cost_estimate=pl.CostEstimate(flops=5 * 10**9, bytes_accessed=4 * 10**6, transcendentals=0),
        name="spread_out",
    )


def look_up(pixels, channels, targets, chunk):
    tiles = targets // LANES
    half = pixels // 2

    def kernel(
        place, own_ref, other_ref, right_ref, spread_hbm, pool_ref, motion_ref,
        out_own, out_other, left, rest, vol, looked, looked_low, weight, spread_ref, sem,
    ):
        spread_copy = pltpu.make_async_copy(spread_hbm, spread_ref, sem)
        spread_copy.start()
        scale = channels**-0.5
        first = place[3]
        left[:half, :] = own_ref[:, :channels]
        left[half:, :] = other_ref[:, :channels]
        rest[:half, :] = own_ref[:, channels:]
        rest[half:, :] = other_ref[:, channels:]
        weight[...] = jnp.zeros(weight.shape, F32)
        for level in range(LEVELS):
            weight[level * LANES : level * LANES + AREA, :] = motion_ref[level * AREA : (level + 1) * AREA, :]
        right = right_ref[...]
        contract_last = (((1,), (1,)), ((), ()))
        pooled = jnp.dot(pool_ref[...], right, preferred_element_type=F32)
        high = pooled.astype(BF16)
        low = (pooled - high.astype(F32)).astype(BF16)
        vol[:, :targets] = lax.dot_general(left[...], right, contract_last, preferred_element_type=F32)
        vol[:, targets:] = lax.dot_general(
            left[...], high, contract_last, preferred_element_type=F32
        ) + lax.dot_general(left[...], low, contract_last, preferred_element_type=F32)

        def step(index, carry):
            rows = pl.ds(pl.multiple_of(index * chunk, chunk), chunk)
            shape = (chunk, LANES)
            lane = iota(shape, 1)
            a_of = lane // SIDE
            b_of = lane - a_of * SIDE - RADIUS
            a_of = a_of - RADIUS
            in_window = lane < AREA
            centers = centers_of(place, rest[rows, :].astype(F32), index, chunk)
            for level in range(LEVELS):
                height, apart, width = LANES >> level, 64 >> level, max(4 >> level, 1)
                row = centers[level][0] + a_of
                col = centers[level][1] + b_of - (first >> level)
                within = col & (apart - 1)
                valid = inside(row, height) & inside(col, 2 * apart) & (within < width) & in_window
                strip = ((col >> (6 - level)) & 1) ^ place[4]
                start, count = ((0, tiles), (tiles, 2), (tiles + 2, 1), (tiles + 2, 1))[level]
                if level == 0:
                    cell = target_of(row, strip, within)
                else:
                    cell = (strip * height + row) * width + within + (64 if level == 3 else 0)
                which = jnp.where(valid, cell >> 7, -1)
                found = jnp.zeros(shape, F32)
                for tile in range(count):
                    at = (start + tile) * LANES
                    picked = take(vol[rows, at : at + LANES], cell)
                    found = jnp.where(which == tile, picked, found)
                found = found * scale
                upper = found.astype(BF16)
                looked[rows, level * LANES : (level + 1) * LANES] = upper
                looked_low[rows, level * LANES : (level + 1) * LANES] = (found - upper.astype(F32)).astype(BF16)
            return carry

        lax.fori_loop(0, pixels // chunk, step, 0)

        weight_high = weight[...].astype(BF16)
        weight_low = (weight[...] - weight_high.astype(F32)).astype(BF16)
        motion = jnp.dot(looked[...], weight_high, preferred_element_type=F32)
        motion = motion + jnp.dot(looked[...], weight_low, preferred_element_type=F32)
        motion = motion + jnp.dot(looked_low[...], weight_high, preferred_element_type=F32)
        spread_copy.wait()
        grad_left = jnp.dot(spread_ref[...], right, preferred_element_type=F32) * scale
        out_own[:, :channels] = motion[:half]
        out_own[:, channels:] = grad_left[:half]
        out_other[:, :channels] = motion[half:].astype(BF16)
        out_other[:, channels:] = grad_left[half:].astype(BF16)

    vmem, hbm = pl.BlockSpec(memory_space=pltpu.VMEM), pl.BlockSpec(memory_space=pltpu.HBM)
    return pl.pallas_call(
        kernel,
        out_shape=(
            jax.ShapeDtypeStruct((half, 2 * channels), F32),
            jax.ShapeDtypeStruct((half, 2 * channels), BF16),
        ),
        in_specs=[pl.BlockSpec(memory_space=pltpu.SMEM)] + [vmem] * 3 + [hbm] + [vmem] * 2,
        out_specs=[vmem] * 2,
        scratch_shapes=[
            pltpu.VMEM((pixels, channels), BF16),
            pltpu.VMEM((pixels, LEVELS * AREA + 2), BF16),
            pltpu.VMEM((pixels, targets + 3 * LANES), F32),
            pltpu.VMEM((pixels, LEVELS * LANES), BF16),
            pltpu.VMEM((pixels, LEVELS * LANES), BF16),
            pltpu.VMEM((LEVELS * LANES, channels), F32),
            pltpu.VMEM((pixels, targets), BF16),
            pltpu.SemaphoreType.DMA,
        ],
        compiler_params=pltpu.CompilerParams(vmem_limit_bytes=24 * 2**20),
        cost_estimate=pl.CostEstimate(flops=6 * 10**9, bytes_accessed=4 * 10**6, transcendentals=0),
        name="look_up",
    )


def add_up(parts, cells, channels, hidden_size):
    def kernel(parts_ref, hidden_ref, context_ref, joined_ref, grad_ref):
        total = parts_ref[0].astype(F32)
        for part in range(1, parts):
            total = total + parts_ref[part].astype(F32)
        joined_ref[:, :hidden_size] = hidden_ref[...]
        joined_ref[:, hidden_size : hidden_size + channels] = jnp.maximum(total[:, :channels], 0.0).astype(BF16)
        joined_ref[:, hidden_size + channels :] = context_ref[...]
        grad_ref[...] = total[:, channels:]

    vmem, hbm = pl.BlockSpec(memory_space=pltpu.VMEM), pl.BlockSpec(memory_space=pltpu.HBM)
    return pl.pallas_call(
        kernel,
        out_shape=(
            jax.ShapeDtypeStruct((cells, 2 * channels), BF16),
            jax.ShapeDtypeStruct((cells, channels), F32),
        ),
        in_specs=[vmem] * 3,
        out_specs=[vmem] * 2,
        compiler_params=pltpu.CompilerParams(vmem_limit_bytes=16 * 2**20),
        name="add_up",
    )


def sum_parts(parts, rows, cols, channels):
    def kernel(parts_ref, out_ref):
        total = parts_ref[0].astype(F32)
        for part in range(1, parts):
            total = total + parts_ref[part].astype(F32)
        for row in range(rows):
            out_ref[row] = total[row * cols : (row + 1) * cols]

    vmem = pl.BlockSpec(memory_space=pltpu.VMEM)
    return pl.pallas_call(
        kernel,
        out_shape=jax.ShapeDtypeStruct((rows, cols, channels), F32),
        in_specs=[vmem],
        out_specs=vmem,
        compiler_params=pltpu.CompilerParams(vmem_limit_bytes=16 * 2**20),
        name="sum_parts",
    )


def warm(*weights):
    def kernel(*refs):
        total = refs[0][0, :16, :LANES]
        for ref in refs[1:-1]:
            total = total + ref[0, :16, :LANES]
        refs[-1][...] = total

    vmem = pl.BlockSpec(memory_space=pltpu.VMEM)
    return pl.pallas_call(
        kernel,
        out_shape=jax.ShapeDtypeStruct((16, LANES), BF16),
        in_specs=[vmem] * len(weights),
        out_specs=vmem,
        compiler_params=pltpu.CompilerParams(vmem_limit_bytes=24 * 2**20),
        cost_estimate=pl.CostEstimate(flops=2 * 10**9, bytes_accessed=4 * 10**6, transcendentals=0),
        name="warm",
    )(*weights)


def gru(tile_rows, tile_cols, hidden_size, taps):
    high, wide = tile_rows + 8, tile_cols + 8

    def sigmoid(x):
        return 1.0 / (1.0 + jnp.exp(-x))

    def kernel(cells_ref, rg_ref, rc_ref, cg_ref, cc_ref, warm_ref, out_ref):
        flat = high * wide
        hidden_bf = cells_ref[:, :, :hidden_size].reshape(flat, hidden_size)
        inputs = cells_ref[:, :, hidden_size:].reshape(flat, -1)
        hidden = hidden_bf.astype(F32)

        def conv_x(source, weight_ref):
            total = None
            for tap in range(taps):
                product = jnp.dot(source, weight_ref[tap], preferred_element_type=F32)
                shift = (2 - tap) % flat
                if shift:
                    product = pltpu.roll(product, shift, 0)
                total = product if total is None else total + product
            return total

        gates = sigmoid(conv_x(jnp.concatenate([hidden_bf, inputs], axis=-1), rg_ref))
        update, reset = gates[:, :hidden_size], gates[:, hidden_size:]
        reset_state = (reset * hidden).astype(BF16)
        candidate = jnp.tanh(conv_x(jnp.concatenate([reset_state, inputs], axis=-1), rc_ref))
        middle = (1.0 - update) * hidden + update * candidate

        def own_columns(values):
            moved = pltpu.roll(values, flat - 4, 0).reshape(high, wide, -1)
            return moved[:, :tile_cols].reshape(high * tile_cols, -1)

        middle_bf = own_columns(middle).astype(BF16)
        inputs = own_columns(inputs.astype(F32)).astype(BF16)
        middle = middle_bf.astype(F32)

        def conv_y(source, weight_ref, count):
            total = None
            for tap in range(taps):
                product = jnp.dot(source, weight_ref[tap], preferred_element_type=F32)
                part = product[tap * tile_cols : (tap + count) * tile_cols]
                total = part if total is None else total + part
            return total

        gates = sigmoid(conv_y(jnp.concatenate([middle_bf, inputs], axis=-1), cg_ref, high - 4))
        reset = gates[:, hidden_size:]
        update = gates[2 * tile_cols : (2 + tile_rows) * tile_cols, :hidden_size]
        reset_state = (reset * middle[2 * tile_cols : (high - 2) * tile_cols]).astype(F32)
        edge = jnp.zeros((2 * tile_cols, hidden_size), F32)
        reset_state = jnp.concatenate([edge, reset_state, edge], axis=0).astype(BF16)
        joined = jnp.concatenate([reset_state, inputs], axis=-1)
        total = None
        for tap in range(taps):
            product = jnp.dot(joined, cc_ref[tap], preferred_element_type=F32)
            part = product[(tap + 2) * tile_cols : (tap + 2 + tile_rows) * tile_cols]
            total = part if total is None else total + part
        candidate = jnp.tanh(total)
        center = middle[4 * tile_cols : (4 + tile_rows) * tile_cols]
        out_ref[...] = (1.0 - update) * center + update * candidate

    return pl.pallas_call(
        kernel,
        out_shape=jax.ShapeDtypeStruct((tile_rows * tile_cols, hidden_size), F32),
        in_specs=[pl.BlockSpec(memory_space=pltpu.VMEM)] * 6,
        out_specs=pl.BlockSpec(memory_space=pltpu.VMEM),
        compiler_params=pltpu.CompilerParams(vmem_limit_bytes=24 * 2**20),
        cost_estimate=pl.CostEstimate(flops=10**9, bytes_accessed=5 * 10**6, transcendentals=10**5),
        name="gru",
    )


def with_halo(cells, axis, dim, width):
    count = lax.axis_size(axis)
    ends = count - 1
    head = lax.slice_in_dim(cells, 0, width, axis=dim)
    tail = lax.slice_in_dim(cells, cells.shape[dim] - width, cells.shape[dim], axis=dim)
    return jnp.concatenate(
        [
            lax.ppermute(tail, axis, [(i, (i + 1) % count) for i in range(ends)]),
            cells,
            lax.ppermute(head, axis, [((i + 1) % count, i) for i in range(ends)]),
        ],
        axis=dim,
    )


def swap(block, axis, bit):
    return lax.ppermute(block, axis, [(i, i ^ bit) for i in range(lax.axis_size(axis))])


ROW = ("yh", "z", "core")
COL = ("x", "yl")
SPREAD = ("yh", "x", "yl")


def shards(
    left_features,
    right_features,
    flow_offsets,
    look_cotangent,
    hidden_state,
    context,
    motion_weight,
    row_gates,
    row_candidate,
    column_gates,
    column_candidate,
):
    tile_rows, tile_cols, channels = left_features.shape
    strip_rows, strip_cols = right_features.shape[:2]
    hidden_size = hidden_state.shape[-1]
    zs = lax.axis_size("z")
    cells = tile_rows * tile_cols
    pixels = 2 * zs * cells
    strip = strip_rows * strip_cols
    targets = lax.axis_size(SPREAD) * strip
    first_col = lax.axis_index(COL) * tile_cols

    place = jnp.stack(
        [
            lax.axis_index("yh") * (tile_rows * 2 * zs),
            first_col,
            lax.axis_index("core"),
            lax.axis_index(("z", "core")) * strip_cols,
            lax.axis_index("yh"),
        ]
    ).astype(I32)
    lefts, right = pack(cells, tile_cols, channels, zs)(
        left_features.reshape(cells, channels),
        look_cotangent.reshape(cells, -1),
        flow_offsets,
        right_features,
    )

    left_cot = lax.all_to_all(lefts, "z", 0, 0).reshape(pixels // 2, -1)
    right = jnp.concatenate([right, swap(right, "yh", 1)], axis=0)
    rights = jnp.broadcast_to(right[None], (lax.axis_size(COL),) + right.shape)
    left_cot, rights = lax.optimization_barrier((left_cot, rights))
    left_cot_other = swap(left_cot, "core", 1)
    right = lax.all_to_all(rights, COL, 0, 0).reshape(targets, channels)

    pool = jnp.asarray(pool_matrix(LANES, 2, strip_cols))
    spread, grad = spread_out(pixels, channels, targets, 64, targets // strip)(place, left_cot, left_cot_other, pool)
    outgoing, outgoing_other = look_up(pixels, channels, targets, 64)(
        place, left_cot, left_cot_other, right, spread, pool, motion_weight
    )

    outgoing = (outgoing + swap(outgoing_other, "core", 1).astype(F32)).astype(BF16)
    parts = lax.all_to_all(outgoing.reshape(zs, cells, 2 * channels), "z", 0, 0)
    parts, grad = lax.optimization_barrier((parts, grad))
    grad = lax.all_to_all(grad, SPREAD, 0, 0)
    grad_right = sum_parts(targets // strip, strip_rows, strip_cols, channels)(grad)

    joined, grad_left = add_up(zs, cells, channels, hidden_size)(
        parts, hidden_state.reshape(cells, hidden_size), context.reshape(cells, -1)
    )
    joined = joined.reshape(tile_rows, tile_cols, -1)
    joined = with_halo(with_halo(joined, ROW, 0, 4), COL, 1, 4)
    new_hidden = gru(tile_rows, tile_cols, hidden_size, row_gates.shape[0])(
        joined, row_gates, row_candidate, column_gates, column_candidate,
        warm(row_gates, row_candidate, column_gates, column_candidate),
    )
    return (
        new_hidden.reshape(hidden_state.shape),
        grad_left.reshape(left_features.shape),
        grad_right,
    )


def solution(mesh):
    mesh = jax.sharding.Mesh(mesh.devices.reshape(2, 8, 2, 4, 4), ROW + COL)
    tiled = P(ROW, COL, None)
    in_specs = (tiled, P(COL, ROW, None), P(None, ROW, None), tiled, tiled, tiled) + (P(),) * 5
    out_specs = (tiled, tiled, P(COL, ROW, None))
    return jax.shard_map(shards, mesh=mesh, in_specs=in_specs, out_specs=out_specs, check_vma=False)
```

time: 545 us -> 114 us (0.21); the launches traced: 537 us -> 113 us
  waiting for transfers between devices: 244 us -> 16.8 us
  blocking collectives: 139 us -> 16.5 us
  matrix products: 55 us -> 0 us
  local copies, waits for them, and re-layouts: 41 us -> 3.99 us
  starting transfers between devices: 33.1 us -> 54.6 us
  Pallas kernels: 0 us -> 19.3 us
  between operations: 14.2 us -> 0.84 us
  other arithmetic: 8.71 us -> 0.9 us
    reduce_scatter x3 -> x0, waiting for transfers between devices: 240 us -> none  [the longest x1 99.6 us: shards(): lax.psum_scatter(grad_right_part, 'row', scatter_dimension=1, tiled=True)]
    all_gather x3 -> x0, blocking collectives: 139 us -> none  [the longest x1 56.7 us: shards(): right_stripe = lax.all_gather(right_features, 'row', axis=1, tiled=True)]
    dot_general x76 -> x0, matrix products: 55 us -> none  [the longest x12 12.9 us: window_block(): inner = jnp.einsum('prc,pbc->prb', current, col_band, precision=highest)]
    all_to_all x0 -> x3, starting transfers between devices: none -> 26.4 us  [the longest x1 10.3 us: shards(): left_cot = lax.all_to_all(lefts, 'z', 0, 0).reshape(pixels // 2, -1)]
    pallas_call x0 -> x7, Pallas kernels: none -> 19.3 us  [the longest x1 6.99 us: shards(): look_up(pixels, channels, targets, 64)]
    all_to_all x0 -> x1, blocking collectives: none -> 16.5 us  [shards(): parts = lax.all_to_all(outgoing.reshape(zs, cells, 2 * channels), 'z', 0, 0)]
    reshape x69 -> x0, local copies, waits for them, and re-layouts: 14.9 us -> none  [the longest x28 5.78 us: window_block(): cot_level = cot_level.reshape(pixel_count, window_side, window_side)]
    ppermute x4 -> x2, starting transfers between devices: 21.1 us -> 11.6 us  [with_halo(): lax.ppermute(head, axis, [((i + 1) % count, i) for i in range(ends)])]
  transfers between devices with their start and end apart: 11 -> 10, of which waited for: 6 -> 6; matrix products, arithmetic and copies ran while one was open for 3% -> 1% of each run, Pallas kernels for 0% -> 8%
where the time goes in v1:
time: 114 us; the launch traced here: 113 us
  starting transfers between devices  54.6 us (48%)
  Pallas kernels  19.3 us (17%)
  waiting for transfers between devices  16.8 us (15%)
  blocking collectives  16.5 us (14%)
  local copies, waits for them, and re-layouts  3.99 us (4%)
    all_to_all x1, blocking collectives, shards(): parts = lax.all_to_all(outgoing.reshape(zs, cells, 2 * channels), 'z', 0, 0)  16.5 us
    ppermute x2, starting transfers between devices, with_halo(): lax.ppermute(head, axis, [((i + 1) % count, i) for i in range(ends)])  11.6 us
    all_to_all x1, starting transfers between devices, shards(): left_cot = lax.all_to_all(lefts, 'z', 0, 0).reshape(pixels // 2, -1)  10.3 us
    ppermute x3, starting transfers between devices, swap(): lax.ppermute(block, axis, [(i, i ^ bit) for i in range(lax.axis_size(axis...  8.66 us
    all_to_all x1, starting transfers between devices, shards(): grad = lax.all_to_all(grad, SPREAD, 0, 0)  8.5 us
    ppermute x2, starting transfers between devices, with_halo(): lax.ppermute(tail, axis, [(i, (i + 1) % count) for i in range(ends)])  7.98 us
    ppermute x3, waiting for transfers between devices, swap(): lax.ppermute(block, axis, [(i, i ^ bit) for i in range(lax.axis_size(axis...  7.9 us
    all_to_all x1, starting transfers between devices, shards(): right = lax.all_to_all(rights, COL, 0, 0).reshape(targets, channels)  7.57 us
  transfers between devices with their start and end apart: 10, of which 6 were waited for; matrix products, arithmetic and copies ran while one was open for 1% of the time, Pallas kernels for 8%

profile of v1, /device:TPU:56, one launch (start us, length us, event | category | flops | bytes accessed | tf_op | source)
XLA Modules:
  0.0 113.0 jit_solution(17655697119655626380)
XLA Ops:
  0.6 0.0 copy-start.9
  0.6 2.4 %pack.1 = (bf16[8,32,582]{2,1,0:T(8,128)(2,1)}, bf16[32,256]{1,0:T(8,128)(2,1)}) custom-call(bf16[32,256]{1,0:T(8,128)(2,1)} %bitcast.28, bf16[32,324]{1,0:T(8,128)(2,1)} %bitcast.26, s32[2,4,128]{2,1,0:T(4,128)} %flow_ref.1, bf16[8,4,256]{2,1,0:T(4,128)(2,1)} %right_ref.1), custom_call_target="tpu_custom_call" | custom-call | tf_op jit(solution)/shard_map/pack/pallas_call | solution.py:491
  3.1 10.3 %all-to-all-start = ((bf16[8,32,582]{2,1,0:T(8,128)(2,1)}), bf16[8,32,582]{2,1,0:T(8,128)(2,1)S(1)}, u32[]{:S(2)}, u32[]{:S(2)}) async-start(bf16[8,32,582]{2,1,0:T(8,128)(2,1)} %get-tuple-element.15), calls=%async_computation | async-start | bytes 655360 | tf_op jit(solution)/shard_map/all_to_all | solution.py:498
  13.4 4.7 %collective-permute-start = (bf16[32,256]{1,0:T(8,128)(2,1)}, bf16[32,256]{1,0:T(8,128)(2,1)S(1)}, u32[]{:S(2)}, u32[]{:S(2)}) collective-permute-start(bf16[32,256]{1,0:T(8,128)(2,1)} %get-tuple-element.16), channel_id=1, source_target_pairs={{0,256},{256,0},{1,257},{257,1},{2,258},{258,2},{3,259},{259,3},{4... | collective-permute-start | bytes 49160 | tf_op jit(solution)/shard_map/ppermute | solution.py:451
  18.1 5.0 %collective-permute-done = bf16[32,256]{1,0:T(8,128)(2,1)S(1)} collective-permute-done((bf16[32,256]{1,0:T(8,128)(2,1)}, bf16[32,256]{1,0:T(8,128)(2,1)S(1)}, u32[]{:S(2)}, u32[]{:S(2)}) %collective-permute-start) | collective-permute-done | bytes 16416 | tf_op jit(solution)/shard_map/ppermute | solution.py:451
  23.1 0.7 pad_maximum_fusion.2
  23.8 2.8 %all-to-all-done = bf16[8,32,582]{2,1,0:T(8,128)(2,1)S(1)} async-done(((bf16[8,32,582]{2,1,0:T(8,128)(2,1)}), bf16[8,32,582]{2,1,0:T(8,128)(2,1)S(1)}, u32[]{:S(2)}, u32[]{:S(2)}) %all-to-all-start) | async-done | bytes 298016 | tf_op jit(solution)/shard_map/all_to_all | solution.py:498
  26.7 0.9 broadcast_in_dim.2
  27.5 7.6 %all-to-all-start.1 = ((bf16[16,64,256]{2,1,0:T(8,128)(2,1)}), bf16[16,64,256]{2,1,0:T(8,128)(2,1)S(1)}, u32[]{:S(2)}, u32[]{:S(2)}) async-start(bf16[16,64,256]{2,1,0:T(8,128)(2,1)} %broadcast_in_dim.2), calls=%async_computation.1 | async-start | bytes 1048576 | tf_op jit(solution)/shard_map/all_to_all | solution.py:503
  35.1 1.9 %collective-permute-start.1 = (bf16[256,582]{1,0:T(8,128)(2,1)S(1)}, bf16[256,582]{1,0:T(8,128)(2,1)S(1)}, u32[]{:S(2)}, u32[]{:S(2)}) collective-permute-start(bf16[256,582]{1,0:T(8,128)(2,1)S(1)} %bitcast.16), channel_id=1, source_target_pairs={{0,16},{16,0},{1,17},{17,1},{2,18},{18,2},{3,19},{19,3},{4,20},{20... | collective-permute-start | bytes 893960 | tf_op jit(solution)/shard_map/ppermute | solution.py:451
  37.0 0.1 stack.23.place
  37.1 1.5 %collective-permute-done.1.other_ref = bf16[256,582]{1,0:T(8,128)(2,1)S(1)} collective-permute-done((bf16[256,582]{1,0:T(8,128)(2,1)S(1)}, bf16[256,582]{1,0:T(8,128)(2,1)S(1)}, u32[]{:S(2)}, u32[]{:S(2)}) %collective-permute-start.1) | collective-permute-done | bytes 298016 | tf_op jit(solution)/shard_map/ppermute | solution.py:451
  38.6 6.4 %spread_out.1 = (bf16[512,1024]{1,0:T(8,128)(2,1)S(1)}, bf16[32,32,256]{2,1,0:T(8,128)(2,1)S(1)}) custom-call(s32[5]{0:T(128)S(1)} %stack.23.place, bf16[256,582]{1,0:T(8,128)(2,1)S(1)} %bitcast.17, bf16[256,582]{1,0:T(8,128)(2,1)S(1)} %collective-permute-done.1.other_ref, bf16[384,1024]{1,0:T(8,128)(2,1)S(1)} %copy-done.9), custom_call_target="tpu_custom_call" | custom-call | flops 5000000000 | bytes 4000000 | tf_op jit(solution)/shard_map/spread_out/pallas_call | solution.py:506
  45.1 0.8 copy-done.5
  45.9 7.0 %look_up.1 = (f32[256,512]{1,0:T(8,128)S(1)}, bf16[256,512]{1,0:T(8,128)(2,1)S(1)}) custom-call(s32[5]{0:T(128)S(1)} %stack.23.place, bf16[256,582]{1,0:T(8,128)(2,1)S(1)} %bitcast.18, bf16[256,582]{1,0:T(8,128)(2,1)S(1)} %collective-permute-done.1.other_ref, bf16[1024,256]{1,0:T(8,128)(2,1)S(1)} %bitcast.15, ...), custom_call_target="tpu_custom_call" | custom-call | flops 6000000000 | bytes 4000000 | tf_op jit(solution)/shard_map/look_up/pallas_call | solution.py:507
  52.9 2.0 %collective-permute-start.2 = (bf16[256,512]{1,0:T(8,128)(2,1)S(1)}, bf16[256,512]{1,0:T(8,128)(2,1)S(1)}, u32[]{:S(2)}, u32[]{:S(2)}) collective-permute-start(bf16[256,512]{1,0:T(8,128)(2,1)S(1)} %get-tuple-element.21), channel_id=1, source_target_pairs={{0,16},{16,0},{1,17},{17,1},{2,18},{18,2},{3,19},{19,3},{4,20},{20... | collective-permute-start | bytes 786440 | tf_op jit(solution)/shard_map/ppermute | solution.py:451
  54.9 1.4 %collective-permute-done.2 = bf16[256,512]{1,0:T(8,128)(2,1)S(1)} collective-permute-done((bf16[256,512]{1,0:T(8,128)(2,1)S(1)}, bf16[256,512]{1,0:T(8,128)(2,1)S(1)}, u32[]{:S(2)}, u32[]{:S(2)}) %collective-permute-start.2) | collective-permute-done | bytes 262176 | tf_op jit(solution)/shard_map/ppermute | solution.py:451
  56.3 0.1 add_convert_fusion
  56.4 16.5 %all_to_all.20.parts_ref = bf16[8,32,512]{2,1,0:T(8,128)(2,1)S(1)} all-to-all(bf16[8,32,512]{2,1,0:T(8,128)(2,1)S(1)} %bitcast.25), channel_id=1, replica_groups=mesh['yh'=2,'z'=8,'core'=2,'x'=4,'yl'=4] {'z'}, dimensions={0} | all-to-all | bytes 524288 | tf_op jit(solution)/shard_map/all_to_all | solution.py:512
  72.9 8.5 %all-to-all-start.3 = ((bf16[32,32,256]{2,1,0:T(8,128)(2,1)}), bf16[32,32,256]{2,1,0:T(8,128)(2,1)S(1)}, u32[]{:S(2)}, u32[]{:S(2)}) async-start(bf16[32,32,256]{2,1,0:T(8,128)(2,1)} %copy-done.5), calls=%async_computation.3 | async-start | bytes 1048576 | tf_op jit(solution)/shard_map/all_to_all | solution.py:514
  81.4 0.6 add_up.1
  82.1 1.9 %collective-permute-start.3 = (bf16[4,8,512]{2,1,0:T(8,128)(2,1)S(1)}, bf16[4,8,512]{2,1,0:T(8,128)(2,1)S(1)}, u32[]{:S(2)}, u32[]{:S(2)}) collective-permute-start(bf16[4,8,512]{2,1,0:T(8,128)(2,1)S(1)} %bitcast.19), channel_id=1, source_target_pairs={{0,16},{16,32},{32,48},{48,64},{64,80},{80,96},{96,112},{112,128},... | collective-permute-start | bytes 98312 | tf_op jit(solution)/shard_map/ppermute | solution.py:442
  84.0 9.7 %collective-permute-start.4 = (bf16[4,8,512]{2,1,0:T(8,128)(2,1)S(1)}, bf16[4,8,512]{2,1,0:T(8,128)(2,1)S(1)}, u32[]{:S(2)}, u32[]{:S(2)}) collective-permute-start(bf16[4,8,512]{2,1,0:T(8,128)(2,1)S(1)} %bitcast.20), channel_id=1, source_target_pairs={{16,0},{32,16},{48,32},{64,48},{80,64},{96,80},{112,96},{128,112},... | collective-permute-start | bytes 98312 | tf_op jit(solution)/shard_map/ppermute | solution.py:444
  93.7 1.6 %collective-permute-done.4 = bf16[4,8,512]{2,1,0:T(8,128)(2,1)S(1)} collective-permute-done((bf16[4,8,512]{2,1,0:T(8,128)(2,1)S(1)}, bf16[4,8,512]{2,1,0:T(8,128)(2,1)S(1)}, u32[]{:S(2)}, u32[]{:S(2)}) %collective-permute-start.4) | collective-permute-done | bytes 32800 | tf_op jit(solution)/shard_map/ppermute | solution.py:444
  95.3 6.1 %collective-permute-start.5 = (bf16[12,4,512]{2,1,0:T(4,128)(2,1)S(1)}, bf16[12,4,512]{2,1,0:T(4,128)(2,1)S(1)}, u32[]{:S(2)}, u32[]{:S(2)}) collective-permute-start(bf16[12,4,512]{2,1,0:T(4,128)(2,1)S(1)} %get-tuple-element.27), channel_id=1, source_target_pairs={{0,1},{1,2},{2,3},{3,4},{4,5},{5,6},{6,7},{7,8},{8,9},{9,10},{10,1... | collective-permute-start | bytes 147464 | tf_op jit(solution)/shard_map/ppermute | solution.py:442
  101.4 1.9 %collective-permute-start.6 = (bf16[12,4,512]{2,1,0:T(4,128)(2,1)S(1)}, bf16[12,4,512]{2,1,0:T(4,128)(2,1)S(1)}, u32[]{:S(2)}, u32[]{:S(2)}) collective-permute-start(bf16[12,4,512]{2,1,0:T(4,128)(2,1)S(1)} %get-tuple-element.28), channel_id=1, source_target_pairs={{1,0},{2,1},{3,2},{4,3},{5,4},{6,5},{7,6},{8,7},{9,8},{10,9},{11,1... | collective-permute-start | bytes 147464 | tf_op jit(solution)/shard_map/ppermute | solution.py:444
  103.3 1.1 copy-done.2
  104.4 1.1 copy-done.4
  105.5 4.5 %collective-permute-done.6 = bf16[12,4,512]{2,1,0:T(4,128)(2,1)S(1)} collective-permute-done((bf16[12,4,512]{2,1,0:T(4,128)(2,1)S(1)}, bf16[12,4,512]{2,1,0:T(4,128)(2,1)S(1)}, u32[]{:S(2)}, u32[]{:S(2)}) %collective-permute-start.6) | collective-permute-done | bytes 49184 | tf_op jit(solution)/shard_map/ppermute | solution.py:444
  110.1 0.1 pad_maximum_fusion.cells_ref
  110.2 2.1 %gru.1 = f32[32,128]{1,0:T(8,128)} custom-call(bf16[12,16,512]{2,1,0:T(8,128)(2,1)S(1)} %pad_maximum_fusion.cells_ref, bf16[5,512,256]{2,1,0:T(8,128)(2,1)S(1)} %copy-done, bf16[5,512,128]{2,1,0:T(8,128)(2,1)S(1)} %copy-done.3, bf16[5,512,256]{2,1,0:T(8,128)(2,1)S(1)} %copy-done.1, bf16[5,512,128]{2,1,0:T(8,128)(2,1)S(1)} %copy-done.4, ...), custom_call_target="tpu_custom_call" | custom-call | flops 1000000000 | bytes 5000000 | tf_op jit(solution)/shard_map/gru/pallas_call | solution.py:522
  112.3 0.7 sum_parts.1
  (23 shorter events, 0.1 us)
Async XLA Ops:
  0.6 38.0 %copy-start.9 = (bf16[384,1024]{1,0:T(8,128)(2,1)S(1)}, bf16[384,1024]{1,0:T(8,128)(2,1)}, u32[]{:S(2)}) copy-start(bf16[384,1024]{1,0:T(8,128)(2,1)} %constant.33.clone.pool_ref) | copy-start | bytes 2359300
  3.1 23.6 %all-to-all-start = ((bf16[8,32,582]{2,1,0:T(8,128)(2,1)}), bf16[8,32,582]{2,1,0:T(8,128)(2,1)S(1)}, u32[]{:S(2)}, u32[]{:S(2)}) async-start(bf16[8,32,582]{2,1,0:T(8,128)(2,1)} %get-tuple-element.15), calls=%async_computation | async-start | bytes 655360 | tf_op jit(solution)/shard_map/all_to_all | solution.py:498
  13.4 9.7 %collective-permute-start = (bf16[32,256]{1,0:T(8,128)(2,1)}, bf16[32,256]{1,0:T(8,128)(2,1)S(1)}, u32[]{:S(2)}, u32[]{:S(2)}) collective-permute-start(bf16[32,256]{1,0:T(8,128)(2,1)} %get-tuple-element.16), channel_id=1, source_target_pairs={{0,256},{256,0},{1,257},{257,1},{2,258},{258,2},{3,259},{259,3},{4... | collective-permute-start | bytes 49160 | tf_op jit(solution)/shard_map/ppermute | solution.py:451
  27.5 18.4 %all-to-all-start.1 = ((bf16[16,64,256]{2,1,0:T(8,128)(2,1)}), bf16[16,64,256]{2,1,0:T(8,128)(2,1)S(1)}, u32[]{:S(2)}, u32[]{:S(2)}) async-start(bf16[16,64,256]{2,1,0:T(8,128)(2,1)} %broadcast_in_dim.2), calls=%async_computation.1 | async-start | bytes 1048576 | tf_op jit(solution)/shard_map/all_to_all | solution.py:503
  35.1 3.5 %collective-permute-start.1 = (bf16[256,582]{1,0:T(8,128)(2,1)S(1)}, bf16[256,582]{1,0:T(8,128)(2,1)S(1)}, u32[]{:S(2)}, u32[]{:S(2)}) collective-permute-start(bf16[256,582]{1,0:T(8,128)(2,1)S(1)} %bitcast.16), channel_id=1, source_target_pairs={{0,16},{16,0},{1,17},{17,1},{2,18},{18,2},{3,19},{19,3},{4,20},{20... | collective-permute-start | bytes 893960 | tf_op jit(solution)/shard_map/ppermute | solution.py:451
  37.1 8.8 %copy-start.8 = (f32[324,256]{1,0:T(8,128)S(1)}, f32[324,256]{1,0:T(8,128)}, u32[]{:S(2)}) copy-start(f32[324,256]{1,0:T(8,128)} %motion_ref.1) | copy-start | bytes 995332
  45.1 0.8 copy-start.5
  52.9 3.4 %collective-permute-start.2 = (bf16[256,512]{1,0:T(8,128)(2,1)S(1)}, bf16[256,512]{1,0:T(8,128)(2,1)S(1)}, u32[]{:S(2)}, u32[]{:S(2)}) collective-permute-start(bf16[256,512]{1,0:T(8,128)(2,1)S(1)} %get-tuple-element.21), channel_id=1, source_target_pairs={{0,16},{16,0},{1,17},{17,1},{2,18},{18,2},{3,19},{19,3},{4,20},{20... | collective-permute-start | bytes 786440 | tf_op jit(solution)/shard_map/ppermute | solution.py:451
  56.3 25.1 %copy-start.6 = (bf16[4,8,128]{2,1,0:T(8,128)(2,1)S(1)}, bf16[4,8,128]{2,1,0:T(8,128)(2,1)}, u32[]{:S(2)}) copy-start(bf16[4,8,128]{2,1,0:T(8,128)(2,1)} %param.16) | copy-start | bytes 24580
  56.3 25.1 %copy-start.7 = (bf16[4,8,128]{2,1,0:T(8,128)(2,1)S(1)}, bf16[4,8,128]{2,1,0:T(8,128)(2,1)}, u32[]{:S(2)}) copy-start(bf16[4,8,128]{2,1,0:T(8,128)(2,1)} %param.17) | copy-start | bytes 24580
  56.3 47.0 %copy-start.1 = (bf16[5,512,256]{2,1,0:T(8,128)(2,1)S(1)}, bf16[5,512,256]{2,1,0:T(8,128)(2,1)}, u32[]{:S(2)}) copy-start(bf16[5,512,256]{2,1,0:T(8,128)(2,1)} %cg_ref.1) | copy-start | bytes 3932164
  56.4 46.9 %copy-start = (bf16[5,512,256]{2,1,0:T(8,128)(2,1)S(1)}, bf16[5,512,256]{2,1,0:T(8,128)(2,1)}, u32[]{:S(2)}) copy-start(bf16[5,512,256]{2,1,0:T(8,128)(2,1)} %rg_ref.1) | copy-start | bytes 3932164
  72.9 39.4 %all-to-all-start.3 = ((bf16[32,32,256]{2,1,0:T(8,128)(2,1)}), bf16[32,32,256]{2,1,0:T(8,128)(2,1)S(1)}, u32[]{:S(2)}, u32[]{:S(2)}) async-start(bf16[32,32,256]{2,1,0:T(8,128)(2,1)} %copy-done.5), calls=%async_computation.3 | async-start | bytes 1048576 | tf_op jit(solution)/shard_map/all_to_all | solution.py:514
  82.1 11.6 %collective-permute-start.3 = (bf16[4,8,512]{2,1,0:T(8,128)(2,1)S(1)}, bf16[4,8,512]{2,1,0:T(8,128)(2,1)S(1)}, u32[]{:S(2)}, u32[]{:S(2)}) collective-permute-start(bf16[4,8,512]{2,1,0:T(8,128)(2,1)S(1)} %bitcast.19), channel_id=1, source_target_pairs={{0,16},{16,32},{32,48},{48,64},{64,80},{80,96},{96,112},{112,128},... | collective-permute-start | bytes 98312 | tf_op jit(solution)/shard_map/ppermute | solution.py:442
  84.0 11.2 %collective-permute-start.4 = (bf16[4,8,512]{2,1,0:T(8,128)(2,1)S(1)}, bf16[4,8,512]{2,1,0:T(8,128)(2,1)S(1)}, u32[]{:S(2)}, u32[]{:S(2)}) collective-permute-start(bf16[4,8,512]{2,1,0:T(8,128)(2,1)S(1)} %bitcast.20), channel_id=1, source_target_pairs={{16,0},{32,16},{48,32},{64,48},{80,64},{96,80},{112,96},{128,112},... | collective-permute-start | bytes 98312 | tf_op jit(solution)/shard_map/ppermute | solution.py:444
  95.3 10.2 %collective-permute-start.5 = (bf16[12,4,512]{2,1,0:T(4,128)(2,1)S(1)}, bf16[12,4,512]{2,1,0:T(4,128)(2,1)S(1)}, u32[]{:S(2)}, u32[]{:S(2)}) collective-permute-start(bf16[12,4,512]{2,1,0:T(4,128)(2,1)S(1)} %get-tuple-element.27), channel_id=1, source_target_pairs={{0,1},{1,2},{2,3},{3,4},{4,5},{5,6},{6,7},{7,8},{8,9},{9,10},{10,1... | collective-permute-start | bytes 147464 | tf_op jit(solution)/shard_map/ppermute | solution.py:442
  101.4 8.7 %collective-permute-start.6 = (bf16[12,4,512]{2,1,0:T(4,128)(2,1)S(1)}, bf16[12,4,512]{2,1,0:T(4,128)(2,1)S(1)}, u32[]{:S(2)}, u32[]{:S(2)}) collective-permute-start(bf16[12,4,512]{2,1,0:T(4,128)(2,1)S(1)} %get-tuple-element.28), channel_id=1, source_target_pairs={{1,0},{2,1},{3,2},{4,3},{5,4},{6,5},{7,6},{8,7},{9,8},{10,9},{11,1... | collective-permute-start | bytes 147464 | tf_op jit(solution)/shard_map/ppermute | solution.py:444
  103.3 1.1 copy-start.2
  104.4 1.1 copy-start.4
  105.5 4.7 %copy-start.3 = (bf16[5,512,128]{2,1,0:T(8,128)(2,1)S(1)}, bf16[5,512,128]{2,1,0:T(8,128)(2,1)}, u32[]{:S(2)}) copy-start(bf16[5,512,128]{2,1,0:T(8,128)(2,1)} %rc_ref.1) | copy-start | bytes 1966084

commit v2 on v1

--- a/solution.py
+++ b/solution.py
@@ -496,8 +496,10 @@
     )
 
     left_cot = lax.all_to_all(lefts, "z", 0, 0).reshape(pixels // 2, -1)
-    right = jnp.concatenate([right, swap(right, "yh", 1)], axis=0)
-    rights = jnp.broadcast_to(right[None], (lax.axis_size(COL),) + right.shape)
+    pair = (right, swap(right, "yh", 1))
+    rights = jnp.concatenate(
+        [jnp.broadcast_to(tile[None], (lax.axis_size(COL),) + tile.shape) for tile in pair], axis=1
+    )
     left_cot, rights = lax.optimization_barrier((left_cot, rights))
     left_cot_other = swap(left_cot, "core", 1)
     right = lax.all_to_all(rights, COL, 0, 0).reshape(targets, channels)
@@ -510,13 +512,12 @@
 
     outgoing = (outgoing + swap(outgoing_other, "core", 1).astype(F32)).astype(BF16)
     parts = lax.all_to_all(outgoing.reshape(zs, cells, 2 * channels), "z", 0, 0)
-    parts, grad = lax.optimization_barrier((parts, grad))
+    joined, grad_left = add_up(zs, cells, channels, hidden_size)(
+        parts, hidden_state.reshape(cells, hidden_size), context.reshape(cells, -1)
+    )
+    joined, grad = lax.optimization_barrier((joined, grad))
     grad = lax.all_to_all(grad, SPREAD, 0, 0)
     grad_right = sum_parts(targets // strip, strip_rows, strip_cols, channels)(grad)
-
-    joined, grad_left = add_up(zs, cells, channels, hidden_size)(
-        parts, hidden_state.reshape(cells, hidden_size), context.reshape(cells, -1)
-    )
     joined = joined.reshape(tile_rows, tile_cols, -1)
     joined = with_halo(with_halo(joined, ROW, 0, 4), COL, 1, 4)
     new_hidden = gru(tile_rows, tile_cols, hidden_size, row_gates.shape[0])(

time: 114 us -> 115 us (level)
  local copies, waits for them, and re-layouts: 3.99 us -> 6.09 us
    unnamed x20 -> x24, local copies, waits for them, and re-layouts: 3 us -> 5.21 us
  transfers between devices with their start and end apart: 10 -> 10, of which waited for: 6 -> 6; matrix products, arithmetic and copies ran while one was open for 1% -> 2% of each run, Pallas kernels for 8% -> 8%
where the time goes in v2:
time: 115 us; the launch traced here: 114 us
  starting transfers between devices  53.8 us (47%)
  Pallas kernels  19.2 us (17%)
  blocking collectives  17.5 us (15%)
  waiting for transfers between devices  15.8 us (14%)
  local copies, waits for them, and re-layouts  6.09 us (5%)
    all_to_all x1, blocking collectives, shards(): parts = lax.all_to_all(outgoing.reshape(zs, cells, 2 * channels), 'z', 0, 0)  17.5 us
    ppermute x2, starting transfers between devices, with_halo(): lax.ppermute(head, axis, [((i + 1) % count, i) for i in range(ends)])  11.6 us
    all_to_all x1, starting transfers between devices, shards(): left_cot = lax.all_to_all(lefts, 'z', 0, 0).reshape(pixels // 2, -1)  10.3 us
    ppermute x3, starting transfers between devices, swap(): lax.ppermute(block, axis, [(i, i ^ bit) for i in range(lax.axis_size(axis...  8.8 us
    ppermute x2, starting transfers between devices, with_halo(): lax.ppermute(tail, axis, [(i, (i + 1) % count) for i in range(ends)])  7.99 us
    ppermute x3, waiting for transfers between devices, swap(): lax.ppermute(block, axis, [(i, i ^ bit) for i in range(lax.axis_size(axis...  7.9 us
    all_to_all x1, starting transfers between devices, shards(): right = lax.all_to_all(rights, COL, 0, 0).reshape(targets, channels)  7.57 us
    all_to_all x1, starting transfers between devices, shards(): grad = lax.all_to_all(grad, SPREAD, 0, 0)  7.52 us
  transfers between devices with their start and end apart: 10, of which 6 were waited for; matrix products, arithmetic and copies ran while one was open for 2% of the time, Pallas kernels for 8%

profile of v2, /device:TPU:56, one launch (start us, length us, event | category | flops | bytes accessed | tf_op | source)
XLA Modules:
  0.0 114.3 jit_solution(18214482535128923798)
XLA Ops:
  0.6 2.3 %pack.1 = (bf16[8,32,582]{2,1,0:T(8,128)(2,1)}, bf16[32,256]{1,0:T(8,128)(2,1)}) custom-call(bf16[32,256]{1,0:T(8,128)(2,1)} %bitcast.28, bf16[32,324]{1,0:T(8,128)(2,1)} %bitcast.26, s32[2,4,128]{2,1,0:T(4,128)} %flow_ref.1, bf16[8,4,256]{2,1,0:T(4,128)(2,1)} %right_ref.1), custom_call_target="tpu_custom_call" | custom-call | tf_op jit(solution)/shard_map/pack/pallas_call | solution.py:491
  3.0 10.3 %all-to-all-start = ((bf16[8,32,582]{2,1,0:T(8,128)(2,1)}), bf16[8,32,582]{2,1,0:T(8,128)(2,1)S(1)}, u32[]{:S(2)}, u32[]{:S(2)}) async-start(bf16[8,32,582]{2,1,0:T(8,128)(2,1)} %get-tuple-element.15), calls=%async_computation | async-start | bytes 655360 | tf_op jit(solution)/shard_map/all_to_all | solution.py:498
  13.3 4.8 %collective-permute-start = (bf16[32,256]{1,0:T(8,128)(2,1)}, bf16[32,256]{1,0:T(8,128)(2,1)S(1)}, u32[]{:S(2)}, u32[]{:S(2)}) collective-permute-start(bf16[32,256]{1,0:T(8,128)(2,1)} %get-tuple-element.16), channel_id=1, source_target_pairs={{0,256},{256,0},{1,257},{257,1},{2,258},{258,2},{3,259},{259,3},{4... | collective-permute-start | bytes 49160 | tf_op jit(solution)/shard_map/ppermute | solution.py:451
  18.2 5.0 %collective-permute-done = bf16[32,256]{1,0:T(8,128)(2,1)S(1)} collective-permute-done((bf16[32,256]{1,0:T(8,128)(2,1)}, bf16[32,256]{1,0:T(8,128)(2,1)S(1)}, u32[]{:S(2)}, u32[]{:S(2)}) %collective-permute-start) | collective-permute-done | bytes 16416 | tf_op jit(solution)/shard_map/ppermute | solution.py:451
  23.2 0.7 broadcast_in_dim.4
  24.0 0.8 pad_maximum_fusion
  24.8 1.8 %all-to-all-done = bf16[8,32,582]{2,1,0:T(8,128)(2,1)S(1)} async-done(((bf16[8,32,582]{2,1,0:T(8,128)(2,1)}), bf16[8,32,582]{2,1,0:T(8,128)(2,1)S(1)}, u32[]{:S(2)}, u32[]{:S(2)}) %all-to-all-start) | async-done | bytes 298016 | tf_op jit(solution)/shard_map/all_to_all | solution.py:498
  26.6 7.6 %all-to-all-start.1 = ((bf16[16,64,256]{2,1,0:T(8,128)(2,1)}), bf16[16,64,256]{2,1,0:T(8,128)(2,1)S(1)}, u32[]{:S(2)}, u32[]{:S(2)}) async-start(bf16[16,64,256]{2,1,0:T(8,128)(2,1)} %pad_maximum_fusion), calls=%async_computation.1 | async-start | bytes 1048576 | tf_op jit(solution)/shard_map/all_to_all | solution.py:505
  34.2 1.9 %collective-permute-start.1 = (bf16[256,582]{1,0:T(8,128)(2,1)S(1)}, bf16[256,582]{1,0:T(8,128)(2,1)S(1)}, u32[]{:S(2)}, u32[]{:S(2)}) collective-permute-start(bf16[256,582]{1,0:T(8,128)(2,1)S(1)} %bitcast.16), channel_id=1, source_target_pairs={{0,16},{16,0},{1,17},{17,1},{2,18},{18,2},{3,19},{19,3},{4,20},{20... | collective-permute-start | bytes 893960 | tf_op jit(solution)/shard_map/ppermute | solution.py:451
  36.1 0.1 stack.23.place
  36.2 1.5 %collective-permute-done.1.other_ref = bf16[256,582]{1,0:T(8,128)(2,1)S(1)} collective-permute-done((bf16[256,582]{1,0:T(8,128)(2,1)S(1)}, bf16[256,582]{1,0:T(8,128)(2,1)S(1)}, u32[]{:S(2)}, u32[]{:S(2)}) %collective-permute-start.1) | collective-permute-done | bytes 298016 | tf_op jit(solution)/shard_map/ppermute | solution.py:451
  37.7 6.4 %spread_out.1 = (bf16[512,1024]{1,0:T(8,128)(2,1)S(1)}, bf16[32,32,256]{2,1,0:T(8,128)(2,1)S(1)}) custom-call(s32[5]{0:T(128)S(1)} %stack.23.place, bf16[256,582]{1,0:T(8,128)(2,1)S(1)} %bitcast.17, bf16[256,582]{1,0:T(8,128)(2,1)S(1)} %collective-permute-done.1.other_ref, bf16[384,1024]{1,0:T(8,128)(2,1)S(1)} %copy-done.9), custom_call_target="tpu_custom_call" | custom-call | flops 5000000000 | bytes 4000000 | tf_op jit(solution)/shard_map/spread_out/pallas_call | solution.py:508
  44.1 0.8 copy-done.5
  44.9 1.0 copy-done.10
  45.9 1.2 %copy-done.11 = bf16[512,1024]{1,0:T(8,128)(2,1)S(1)} copy-done((bf16[512,1024]{1,0:T(8,128)(2,1)S(1)}, bf16[512,1024]{1,0:T(8,128)(2,1)}, u32[]{:S(2)}) %copy-start.11) | copy-done | bytes 1048600
  47.1 7.0 %look_up.1 = (f32[256,512]{1,0:T(8,128)S(1)}, bf16[256,512]{1,0:T(8,128)(2,1)S(1)}) custom-call(s32[5]{0:T(128)S(1)} %stack.23.place, bf16[256,582]{1,0:T(8,128)(2,1)S(1)} %bitcast.18, bf16[256,582]{1,0:T(8,128)(2,1)S(1)} %collective-permute-done.1.other_ref, bf16[1024,256]{1,0:T(8,128)(2,1)S(1)} %bitcast.15, bf16[512,1024]{1,0:T(8,128)(2,1)S(1)} %copy-done.11, ...), custom_call_target="tpu_custom_call" | custom-call | flops 6000000000 | bytes 4000000 | tf_op jit(solution)/shard_map/look_up/pallas_call | solution.py:509
  54.2 2.0 %collective-permute-start.2 = (bf16[256,512]{1,0:T(8,128)(2,1)S(1)}, bf16[256,512]{1,0:T(8,128)(2,1)S(1)}, u32[]{:S(2)}, u32[]{:S(2)}) collective-permute-start(bf16[256,512]{1,0:T(8,128)(2,1)S(1)} %get-tuple-element.21), channel_id=1, source_target_pairs={{0,16},{16,0},{1,17},{17,1},{2,18},{18,2},{3,19},{19,3},{4,20},{20... | collective-permute-start | bytes 786440 | tf_op jit(solution)/shard_map/ppermute | solution.py:451
  56.2 1.4 %collective-permute-done.2 = bf16[256,512]{1,0:T(8,128)(2,1)S(1)} collective-permute-done((bf16[256,512]{1,0:T(8,128)(2,1)S(1)}, bf16[256,512]{1,0:T(8,128)(2,1)S(1)}, u32[]{:S(2)}, u32[]{:S(2)}) %collective-permute-start.2) | collective-permute-done | bytes 262176 | tf_op jit(solution)/shard_map/ppermute | solution.py:451
  57.7 17.5 %all_to_all.20.parts_ref = bf16[8,32,512]{2,1,0:T(8,128)(2,1)S(1)} all-to-all(bf16[8,32,512]{2,1,0:T(8,128)(2,1)S(1)} %bitcast.25), channel_id=1, replica_groups=mesh['yh'=2,'z'=8,'core'=2,'x'=4,'yl'=4] {'z'}, dimensions={0} | all-to-all | bytes 524288 | tf_op jit(solution)/shard_map/all_to_all | solution.py:514
  75.2 0.6 add_up.1
  75.9 7.5 %all-to-all-start.3 = ((bf16[32,32,256]{2,1,0:T(8,128)(2,1)}), bf16[32,32,256]{2,1,0:T(8,128)(2,1)S(1)}, u32[]{:S(2)}, u32[]{:S(2)}) async-start(bf16[32,32,256]{2,1,0:T(8,128)(2,1)} %copy-done.5), calls=%async_computation.3 | async-start | bytes 1048576 | tf_op jit(solution)/shard_map/all_to_all | solution.py:519
  83.4 1.9 %collective-permute-start.3 = (bf16[4,8,512]{2,1,0:T(8,128)(2,1)S(1)}, bf16[4,8,512]{2,1,0:T(8,128)(2,1)S(1)}, u32[]{:S(2)}, u32[]{:S(2)}) collective-permute-start(bf16[4,8,512]{2,1,0:T(8,128)(2,1)S(1)} %bitcast.19), channel_id=1, source_target_pairs={{0,16},{16,32},{32,48},{48,64},{64,80},{80,96},{96,112},{112,128},... | collective-permute-start | bytes 98312 | tf_op jit(solution)/shard_map/ppermute | solution.py:442
  85.3 9.7 %collective-permute-start.4 = (bf16[4,8,512]{2,1,0:T(8,128)(2,1)S(1)}, bf16[4,8,512]{2,1,0:T(8,128)(2,1)S(1)}, u32[]{:S(2)}, u32[]{:S(2)}) collective-permute-start(bf16[4,8,512]{2,1,0:T(8,128)(2,1)S(1)} %bitcast.20), channel_id=1, source_target_pairs={{16,0},{32,16},{48,32},{64,48},{80,64},{96,80},{112,96},{128,112},... | collective-permute-start | bytes 98312 | tf_op jit(solution)/shard_map/ppermute | solution.py:444
  95.0 1.6 %collective-permute-done.4 = bf16[4,8,512]{2,1,0:T(8,128)(2,1)S(1)} collective-permute-done((bf16[4,8,512]{2,1,0:T(8,128)(2,1)S(1)}, bf16[4,8,512]{2,1,0:T(8,128)(2,1)S(1)}, u32[]{:S(2)}, u32[]{:S(2)}) %collective-permute-start.4) | collective-permute-done | bytes 32800 | tf_op jit(solution)/shard_map/ppermute | solution.py:444
  96.6 6.1 %collective-permute-start.5 = (bf16[12,4,512]{2,1,0:T(4,128)(2,1)S(1)}, bf16[12,4,512]{2,1,0:T(4,128)(2,1)S(1)}, u32[]{:S(2)}, u32[]{:S(2)}) collective-permute-start(bf16[12,4,512]{2,1,0:T(4,128)(2,1)S(1)} %get-tuple-element.27), channel_id=1, source_target_pairs={{0,1},{1,2},{2,3},{3,4},{4,5},{5,6},{6,7},{7,8},{8,9},{9,10},{10,1... | collective-permute-start | bytes 147464 | tf_op jit(solution)/shard_map/ppermute | solution.py:442
  102.7 1.9 %collective-permute-start.6 = (bf16[12,4,512]{2,1,0:T(4,128)(2,1)S(1)}, bf16[12,4,512]{2,1,0:T(4,128)(2,1)S(1)}, u32[]{:S(2)}, u32[]{:S(2)}) collective-permute-start(bf16[12,4,512]{2,1,0:T(4,128)(2,1)S(1)} %get-tuple-element.28), channel_id=1, source_target_pairs={{1,0},{2,1},{3,2},{4,3},{5,4},{6,5},{7,6},{8,7},{9,8},{10,9},{11,1... | collective-permute-start | bytes 147464 | tf_op jit(solution)/shard_map/ppermute | solution.py:444
  104.7 1.1 copy-done.2
  105.7 1.1 copy-done.4
  106.8 4.5 %collective-permute-done.6 = bf16[12,4,512]{2,1,0:T(4,128)(2,1)S(1)} collective-permute-done((bf16[12,4,512]{2,1,0:T(4,128)(2,1)S(1)}, bf16[12,4,512]{2,1,0:T(4,128)(2,1)S(1)}, u32[]{:S(2)}, u32[]{:S(2)}) %collective-permute-start.6) | collective-permute-done | bytes 49184 | tf_op jit(solution)/shard_map/ppermute | solution.py:444
  111.4 0.1 pad_maximum_fusion.1.cells_ref
  111.5 2.1 %gru.1 = f32[32,128]{1,0:T(8,128)} custom-call(bf16[12,16,512]{2,1,0:T(8,128)(2,1)S(1)} %pad_maximum_fusion.1.cells_ref, bf16[5,512,256]{2,1,0:T(8,128)(2,1)S(1)} %copy-done, bf16[5,512,128]{2,1,0:T(8,128)(2,1)S(1)} %copy-done.3, bf16[5,512,256]{2,1,0:T(8,128)(2,1)S(1)} %copy-done.1, bf16[5,512,128]{2,1,0:T(8,128)(2,1)S(1)} %copy-done.4, ...), custom_call_target="tpu_custom_call" | custom-call | flops 1000000000 | bytes 5000000 | tf_op jit(solution)/shard_map/gru/pallas_call | solution.py:523
  113.6 0.7 sum_parts.1
  (28 shorter events, 0.2 us)
Async XLA Ops:
  3.0 23.6 %all-to-all-start = ((bf16[8,32,582]{2,1,0:T(8,128)(2,1)}), bf16[8,32,582]{2,1,0:T(8,128)(2,1)S(1)}, u32[]{:S(2)}, u32[]{:S(2)}) async-start(bf16[8,32,582]{2,1,0:T(8,128)(2,1)} %get-tuple-element.15), calls=%async_computation | async-start | bytes 655360 | tf_op jit(solution)/shard_map/all_to_all | solution.py:498
  13.3 24.4 %copy-start.9 = (bf16[384,1024]{1,0:T(8,128)(2,1)S(1)}, bf16[384,1024]{1,0:T(8,128)(2,1)}, u32[]{:S(2)}) copy-start(bf16[384,1024]{1,0:T(8,128)(2,1)} %constant.33.clone.pool_ref) | copy-start | bytes 2359300
  13.3 9.9 %collective-permute-start = (bf16[32,256]{1,0:T(8,128)(2,1)}, bf16[32,256]{1,0:T(8,128)(2,1)S(1)}, u32[]{:S(2)}, u32[]{:S(2)}) collective-permute-start(bf16[32,256]{1,0:T(8,128)(2,1)} %get-tuple-element.16), channel_id=1, source_target_pairs={{0,256},{256,0},{1,257},{257,1},{2,258},{258,2},{3,259},{259,3},{4... | collective-permute-start | bytes 49160 | tf_op jit(solution)/shard_map/ppermute | solution.py:451
  26.6 19.3 %all-to-all-start.1 = ((bf16[16,64,256]{2,1,0:T(8,128)(2,1)}), bf16[16,64,256]{2,1,0:T(8,128)(2,1)S(1)}, u32[]{:S(2)}, u32[]{:S(2)}) async-start(bf16[16,64,256]{2,1,0:T(8,128)(2,1)} %pad_maximum_fusion), calls=%async_computation.1 | async-start | bytes 1048576 | tf_op jit(solution)/shard_map/all_to_all | solution.py:505
  34.2 3.5 %collective-permute-start.1 = (bf16[256,582]{1,0:T(8,128)(2,1)S(1)}, bf16[256,582]{1,0:T(8,128)(2,1)S(1)}, u32[]{:S(2)}, u32[]{:S(2)}) collective-permute-start(bf16[256,582]{1,0:T(8,128)(2,1)S(1)} %bitcast.16), channel_id=1, source_target_pairs={{0,16},{16,0},{1,17},{17,1},{2,18},{18,2},{3,19},{19,3},{4,20},{20... | collective-permute-start | bytes 893960 | tf_op jit(solution)/shard_map/ppermute | solution.py:451
  36.2 9.7 %copy-start.8 = (f32[324,256]{1,0:T(8,128)S(1)}, f32[324,256]{1,0:T(8,128)}, u32[]{:S(2)}) copy-start(f32[324,256]{1,0:T(8,128)} %motion_ref.1) | copy-start | bytes 995332
  44.1 0.8 copy-start.5
  44.9 1.0 copy-start.10
  45.9 1.2 %copy-start.11 = (bf16[512,1024]{1,0:T(8,128)(2,1)S(1)}, bf16[512,1024]{1,0:T(8,128)(2,1)}, u32[]{:S(2)}) copy-start(bf16[512,1024]{1,0:T(8,128)(2,1)} %copy-done.10) | copy-start | bytes 3145732
  54.1 21.1 %copy-start.6 = (bf16[4,8,128]{2,1,0:T(8,128)(2,1)S(1)}, bf16[4,8,128]{2,1,0:T(8,128)(2,1)}, u32[]{:S(2)}) copy-start(bf16[4,8,128]{2,1,0:T(8,128)(2,1)} %param.16) | copy-start | bytes 24580
  54.1 21.1 %copy-start.7 = (bf16[4,8,128]{2,1,0:T(8,128)(2,1)S(1)}, bf16[4,8,128]{2,1,0:T(8,128)(2,1)}, u32[]{:S(2)}) copy-start(bf16[4,8,128]{2,1,0:T(8,128)(2,1)} %param.17) | copy-start | bytes 24580
  54.2 3.4 %collective-permute-start.2 = (bf16[256,512]{1,0:T(8,128)(2,1)S(1)}, bf16[256,512]{1,0:T(8,128)(2,1)S(1)}, u32[]{:S(2)}, u32[]{:S(2)}) collective-permute-start(bf16[256,512]{1,0:T(8,128)(2,1)S(1)} %get-tuple-element.21), channel_id=1, source_target_pairs={{0,16},{16,0},{1,17},{17,1},{2,18},{18,2},{3,19},{19,3},{4,20},{20... | collective-permute-start | bytes 786440 | tf_op jit(solution)/shard_map/ppermute | solution.py:451
  57.6 47.1 %copy-start.1 = (bf16[5,512,256]{2,1,0:T(8,128)(2,1)S(1)}, bf16[5,512,256]{2,1,0:T(8,128)(2,1)}, u32[]{:S(2)}) copy-start(bf16[5,512,256]{2,1,0:T(8,128)(2,1)} %cg_ref.1) | copy-start | bytes 3932164
  57.7 47.0 %copy-start = (bf16[5,512,256]{2,1,0:T(8,128)(2,1)S(1)}, bf16[5,512,256]{2,1,0:T(8,128)(2,1)}, u32[]{:S(2)}) copy-start(bf16[5,512,256]{2,1,0:T(8,128)(2,1)} %rg_ref.1) | copy-start | bytes 3932164
  75.9 37.8 %all-to-all-start.3 = ((bf16[32,32,256]{2,1,0:T(8,128)(2,1)}), bf16[32,32,256]{2,1,0:T(8,128)(2,1)S(1)}, u32[]{:S(2)}, u32[]{:S(2)}) async-start(bf16[32,32,256]{2,1,0:T(8,128)(2,1)} %copy-done.5), calls=%async_computation.3 | async-start | bytes 1048576 | tf_op jit(solution)/shard_map/all_to_all | solution.py:519
  83.4 11.6 %collective-permute-start.3 = (bf16[4,8,512]{2,1,0:T(8,128)(2,1)S(1)}, bf16[4,8,512]{2,1,0:T(8,128)(2,1)S(1)}, u32[]{:S(2)}, u32[]{:S(2)}) collective-permute-start(bf16[4,8,512]{2,1,0:T(8,128)(2,1)S(1)} %bitcast.19), channel_id=1, source_target_pairs={{0,16},{16,32},{32,48},{48,64},{64,80},{80,96},{96,112},{112,128},... | collective-permute-start | bytes 98312 | tf_op jit(solution)/shard_map/ppermute | solution.py:442
  85.3 11.2 %collective-permute-start.4 = (bf16[4,8,512]{2,1,0:T(8,128)(2,1)S(1)}, bf16[4,8,512]{2,1,0:T(8,128)(2,1)S(1)}, u32[]{:S(2)}, u32[]{:S(2)}) collective-permute-start(bf16[4,8,512]{2,1,0:T(8,128)(2,1)S(1)} %bitcast.20), channel_id=1, source_target_pairs={{16,0},{32,16},{48,32},{64,48},{80,64},{96,80},{112,96},{128,112},... | collective-permute-start | bytes 98312 | tf_op jit(solution)/shard_map/ppermute | solution.py:444
  96.6 10.2 %collective-permute-start.5 = (bf16[12,4,512]{2,1,0:T(4,128)(2,1)S(1)}, bf16[12,4,512]{2,1,0:T(4,128)(2,1)S(1)}, u32[]{:S(2)}, u32[]{:S(2)}) collective-permute-start(bf16[12,4,512]{2,1,0:T(4,128)(2,1)S(1)} %get-tuple-element.27), channel_id=1, source_target_pairs={{0,1},{1,2},{2,3},{3,4},{4,5},{5,6},{6,7},{7,8},{8,9},{9,10},{10,1... | collective-permute-start | bytes 147464 | tf_op jit(solution)/shard_map/ppermute | solution.py:442
  102.7 8.7 %collective-permute-start.6 = (bf16[12,4,512]{2,1,0:T(4,128)(2,1)S(1)}, bf16[12,4,512]{2,1,0:T(4,128)(2,1)S(1)}, u32[]{:S(2)}, u32[]{:S(2)}) collective-permute-start(bf16[12,4,512]{2,1,0:T(4,128)(2,1)S(1)} %get-tuple-element.28), channel_id=1, source_target_pairs={{1,0},{2,1},{3,2},{4,3},{5,4},{6,5},{7,6},{8,7},{9,8},{10,9},{11,1... | collective-permute-start | bytes 147464 | tf_op jit(solution)/shard_map/ppermute | solution.py:444
  104.7 1.1 copy-start.2
  105.7 1.1 copy-start.4
  106.8 4.7 %copy-start.3 = (bf16[5,512,128]{2,1,0:T(8,128)(2,1)S(1)}, bf16[5,512,128]{2,1,0:T(8,128)(2,1)}, u32[]{:S(2)}) copy-start(bf16[5,512,128]{2,1,0:T(8,128)(2,1)} %rc_ref.1) | copy-start | bytes 1966084

commit v3 on v2

--- a/solution.py
+++ b/solution.py
@@ -505,19 +505,20 @@
     right = lax.all_to_all(rights, COL, 0, 0).reshape(targets, channels)
 
     pool = jnp.asarray(pool_matrix(LANES, 2, strip_cols))
-    spread, grad = spread_out(pixels, channels, targets, 64, targets // strip)(place, left_cot, left_cot_other, pool)
-    outgoing, outgoing_other = look_up(pixels, channels, targets, 64)(
+    spread, grad = spread_out(pixels, channels, targets, 32, targets // strip)(place, left_cot, left_cot_other, pool)
+    outgoing, outgoing_other = look_up(pixels, channels, targets, 32)(
         place, left_cot, left_cot_other, right, spread, pool, motion_weight
     )
 
     outgoing = (outgoing + swap(outgoing_other, "core", 1).astype(F32)).astype(BF16)
     parts = lax.all_to_all(outgoing.reshape(zs, cells, 2 * channels), "z", 0, 0)
+    parts, grad = lax.optimization_barrier((parts, grad))
+    grad = lax.all_to_all(grad, SPREAD, 0, 0)
+    grad_right = sum_parts(targets // strip, strip_rows, strip_cols, channels)(grad)
+
     joined, grad_left = add_up(zs, cells, channels, hidden_size)(
         parts, hidden_state.reshape(cells, hidden_size), context.reshape(cells, -1)
     )
-    joined, grad = lax.optimization_barrier((joined, grad))
-    grad = lax.all_to_all(grad, SPREAD, 0, 0)
-    grad_right = sum_parts(targets // strip, strip_rows, strip_cols, channels)(grad)
     joined = joined.reshape(tile_rows, tile_cols, -1)
     joined = with_halo(with_halo(joined, ROW, 0, 4), COL, 1, 4)
     new_hidden = gru(tile_rows, tile_cols, hidden_size, row_gates.shape[0])(

time: 115 us -> 115 us (level)
  Pallas kernels: 19.2 us -> 21.6 us
  local copies, waits for them, and re-layouts: 6.09 us -> 3.88 us
    pallas_call x2, Pallas kernels: 13.4 us -> 15.8 us  [the longest x1 8.23 us: shards(): look_up(pixels, channels, targets, 32)]
    unnamed x24 -> x20, local copies, waits for them, and re-layouts: 5.21 us -> 3 us
  transfers between devices with their start and end apart: 10 -> 10, of which waited for: 6 -> 6; matrix products, arithmetic and copies ran while one was open for 2% -> 2% of each run, Pallas kernels for 8% -> 9%
where the time goes in v3:
time: 115 us; the launch traced here: 114 us
  starting transfers between devices  53.6 us (47%)
  Pallas kernels  21.6 us (19%)
  blocking collectives  17.5 us (15%)
  waiting for transfers between devices  15.8 us (14%)
  local copies, waits for them, and re-layouts  3.88 us (3%)
    all_to_all x1, blocking collectives, shards(): parts = lax.all_to_all(outgoing.reshape(zs, cells, 2 * channels), 'z', 0, 0)  17.5 us
    ppermute x2, starting transfers between devices, with_halo(): lax.ppermute(head, axis, [((i + 1) % count, i) for i in range(ends)])  11.6 us
    all_to_all x1, starting transfers between devices, shards(): left_cot = lax.all_to_all(lefts, 'z', 0, 0).reshape(pixels // 2, -1)  10.3 us
    ppermute x3, starting transfers between devices, swap(): lax.ppermute(block, axis, [(i, i ^ bit) for i in range(lax.axis_size(axis...  8.8 us
    pallas_call x1, Pallas kernels, shards(): look_up(pixels, channels, targets, 32)  8.23 us
    ppermute x2, starting transfers between devices, with_halo(): lax.ppermute(tail, axis, [(i, (i + 1) % count) for i in range(ends)])  7.98 us
    ppermute x3, waiting for transfers between devices, swap(): lax.ppermute(block, axis, [(i, i ^ bit) for i in range(lax.axis_size(axis...  7.9 us
    pallas_call x1, Pallas kernels, shards(): spread_out(pixels, channels, targets, 32, targets // strip)  7.59 us
  transfers between devices with their start and end apart: 10, of which 6 were waited for; matrix products, arithmetic and copies ran while one was open for 2% of the time, Pallas kernels for 9%

profile of v3, /device:TPU:56, one launch (start us, length us, event | category | flops | bytes accessed | tf_op | source)
XLA Modules:
  0.0 114.4 jit_solution(554665419084439962)
XLA Ops:
  0.6 2.4 %pack.1 = (bf16[8,32,582]{2,1,0:T(8,128)(2,1)}, bf16[32,256]{1,0:T(8,128)(2,1)}) custom-call(bf16[32,256]{1,0:T(8,128)(2,1)} %bitcast.28, bf16[32,324]{1,0:T(8,128)(2,1)} %bitcast.26, s32[2,4,128]{2,1,0:T(4,128)} %flow_ref.1, bf16[8,4,256]{2,1,0:T(4,128)(2,1)} %right_ref.1), custom_call_target="tpu_custom_call" | custom-call | tf_op jit(solution)/shard_map/pack/pallas_call | solution.py:491
  3.0 10.3 %all-to-all-start = ((bf16[8,32,582]{2,1,0:T(8,128)(2,1)}), bf16[8,32,582]{2,1,0:T(8,128)(2,1)S(1)}, u32[]{:S(2)}, u32[]{:S(2)}) async-start(bf16[8,32,582]{2,1,0:T(8,128)(2,1)} %get-tuple-element.15), calls=%async_computation | async-start | bytes 655360 | tf_op jit(solution)/shard_map/all_to_all | solution.py:498
  13.3 4.8 %collective-permute-start = (bf16[32,256]{1,0:T(8,128)(2,1)}, bf16[32,256]{1,0:T(8,128)(2,1)S(1)}, u32[]{:S(2)}, u32[]{:S(2)}) collective-permute-start(bf16[32,256]{1,0:T(8,128)(2,1)} %get-tuple-element.16), channel_id=1, source_target_pairs={{0,256},{256,0},{1,257},{257,1},{2,258},{258,2},{3,259},{259,3},{4... | collective-permute-start | bytes 49160 | tf_op jit(solution)/shard_map/ppermute | solution.py:451
  18.2 5.0 %collective-permute-done = bf16[32,256]{1,0:T(8,128)(2,1)S(1)} collective-permute-done((bf16[32,256]{1,0:T(8,128)(2,1)}, bf16[32,256]{1,0:T(8,128)(2,1)S(1)}, u32[]{:S(2)}, u32[]{:S(2)}) %collective-permute-start) | collective-permute-done | bytes 16416 | tf_op jit(solution)/shard_map/ppermute | solution.py:451
  23.2 0.7 broadcast_in_dim.4
  24.0 0.8 pad_maximum_fusion
  24.8 1.8 %all-to-all-done = bf16[8,32,582]{2,1,0:T(8,128)(2,1)S(1)} async-done(((bf16[8,32,582]{2,1,0:T(8,128)(2,1)}), bf16[8,32,582]{2,1,0:T(8,128)(2,1)S(1)}, u32[]{:S(2)}, u32[]{:S(2)}) %all-to-all-start) | async-done | bytes 298016 | tf_op jit(solution)/shard_map/all_to_all | solution.py:498
  26.6 7.6 %all-to-all-start.1 = ((bf16[16,64,256]{2,1,0:T(8,128)(2,1)}), bf16[16,64,256]{2,1,0:T(8,128)(2,1)S(1)}, u32[]{:S(2)}, u32[]{:S(2)}) async-start(bf16[16,64,256]{2,1,0:T(8,128)(2,1)} %pad_maximum_fusion), calls=%async_computation.1 | async-start | bytes 1048576 | tf_op jit(solution)/shard_map/all_to_all | solution.py:505
  34.2 1.9 %collective-permute-start.1 = (bf16[256,582]{1,0:T(8,128)(2,1)S(1)}, bf16[256,582]{1,0:T(8,128)(2,1)S(1)}, u32[]{:S(2)}, u32[]{:S(2)}) collective-permute-start(bf16[256,582]{1,0:T(8,128)(2,1)S(1)} %bitcast.16), channel_id=1, source_target_pairs={{0,16},{16,0},{1,17},{17,1},{2,18},{18,2},{3,19},{19,3},{4,20},{20... | collective-permute-start | bytes 893960 | tf_op jit(solution)/shard_map/ppermute | solution.py:451
  36.1 0.1 stack.23.place
  36.2 1.5 %collective-permute-done.1.other_ref = bf16[256,582]{1,0:T(8,128)(2,1)S(1)} collective-permute-done((bf16[256,582]{1,0:T(8,128)(2,1)S(1)}, bf16[256,582]{1,0:T(8,128)(2,1)S(1)}, u32[]{:S(2)}, u32[]{:S(2)}) %collective-permute-start.1) | collective-permute-done | bytes 298016 | tf_op jit(solution)/shard_map/ppermute | solution.py:451
  37.7 7.6 %spread_out.1 = (bf16[512,1024]{1,0:T(8,128)(2,1)S(1)}, bf16[32,32,256]{2,1,0:T(8,128)(2,1)S(1)}) custom-call(s32[5]{0:T(128)S(1)} %stack.23.place, bf16[256,582]{1,0:T(8,128)(2,1)S(1)} %bitcast.17, bf16[256,582]{1,0:T(8,128)(2,1)S(1)} %collective-permute-done.1.other_ref, bf16[384,1024]{1,0:T(8,128)(2,1)S(1)} %copy-done.9), custom_call_target="tpu_custom_call" | custom-call | flops 5000000000 | bytes 4000000 | tf_op jit(solution)/shard_map/spread_out/pallas_call | solution.py:508
  45.3 0.8 copy-done.5
  46.1 8.2 %look_up.1 = (f32[256,512]{1,0:T(8,128)S(1)}, bf16[256,512]{1,0:T(8,128)(2,1)S(1)}) custom-call(s32[5]{0:T(128)S(1)} %stack.23.place, bf16[256,582]{1,0:T(8,128)(2,1)S(1)} %bitcast.18, bf16[256,582]{1,0:T(8,128)(2,1)S(1)} %collective-permute-done.1.other_ref, bf16[1024,256]{1,0:T(8,128)(2,1)S(1)} %bitcast.15, ...), custom_call_target="tpu_custom_call" | custom-call | flops 6000000000 | bytes 4000000 | tf_op jit(solution)/shard_map/look_up/pallas_call | solution.py:509
  54.3 2.0 %collective-permute-start.2 = (bf16[256,512]{1,0:T(8,128)(2,1)S(1)}, bf16[256,512]{1,0:T(8,128)(2,1)S(1)}, u32[]{:S(2)}, u32[]{:S(2)}) collective-permute-start(bf16[256,512]{1,0:T(8,128)(2,1)S(1)} %get-tuple-element.21), channel_id=1, source_target_pairs={{0,16},{16,0},{1,17},{17,1},{2,18},{18,2},{3,19},{19,3},{4,20},{20... | collective-permute-start | bytes 786440 | tf_op jit(solution)/shard_map/ppermute | solution.py:451
  56.4 1.4 %collective-permute-done.2 = bf16[256,512]{1,0:T(8,128)(2,1)S(1)} collective-permute-done((bf16[256,512]{1,0:T(8,128)(2,1)S(1)}, bf16[256,512]{1,0:T(8,128)(2,1)S(1)}, u32[]{:S(2)}, u32[]{:S(2)}) %collective-permute-start.2) | collective-permute-done | bytes 262176 | tf_op jit(solution)/shard_map/ppermute | solution.py:451
  57.8 0.1 add_convert_fusion
  57.8 0.0 copy-start
  57.9 17.5 %all_to_all.20.parts_ref = bf16[8,32,512]{2,1,0:T(8,128)(2,1)S(1)} all-to-all(bf16[8,32,512]{2,1,0:T(8,128)(2,1)S(1)} %bitcast.25), channel_id=1, replica_groups=mesh['yh'=2,'z'=8,'core'=2,'x'=4,'yl'=4] {'z'}, dimensions={0} | all-to-all | bytes 524288 | tf_op jit(solution)/shard_map/all_to_all | solution.py:514
  75.4 7.4 %all-to-all-start.3 = ((bf16[32,32,256]{2,1,0:T(8,128)(2,1)}), bf16[32,32,256]{2,1,0:T(8,128)(2,1)S(1)}, u32[]{:S(2)}, u32[]{:S(2)}) async-start(bf16[32,32,256]{2,1,0:T(8,128)(2,1)} %copy-done.5), calls=%async_computation.3 | async-start | bytes 1048576 | tf_op jit(solution)/shard_map/all_to_all | solution.py:516
  82.8 0.6 add_up.1
  83.4 1.9 %collective-permute-start.3 = (bf16[4,8,512]{2,1,0:T(8,128)(2,1)S(1)}, bf16[4,8,512]{2,1,0:T(8,128)(2,1)S(1)}, u32[]{:S(2)}, u32[]{:S(2)}) collective-permute-start(bf16[4,8,512]{2,1,0:T(8,128)(2,1)S(1)} %bitcast.19), channel_id=1, source_target_pairs={{0,16},{16,32},{32,48},{48,64},{64,80},{80,96},{96,112},{112,128},... | collective-permute-start | bytes 98312 | tf_op jit(solution)/shard_map/ppermute | solution.py:442
  85.3 9.7 %collective-permute-start.4 = (bf16[4,8,512]{2,1,0:T(8,128)(2,1)S(1)}, bf16[4,8,512]{2,1,0:T(8,128)(2,1)S(1)}, u32[]{:S(2)}, u32[]{:S(2)}) collective-permute-start(bf16[4,8,512]{2,1,0:T(8,128)(2,1)S(1)} %bitcast.20), channel_id=1, source_target_pairs={{16,0},{32,16},{48,32},{64,48},{80,64},{96,80},{112,96},{128,112},... | collective-permute-start | bytes 98312 | tf_op jit(solution)/shard_map/ppermute | solution.py:444
  95.0 1.6 %collective-permute-done.4 = bf16[4,8,512]{2,1,0:T(8,128)(2,1)S(1)} collective-permute-done((bf16[4,8,512]{2,1,0:T(8,128)(2,1)S(1)}, bf16[4,8,512]{2,1,0:T(8,128)(2,1)S(1)}, u32[]{:S(2)}, u32[]{:S(2)}) %collective-permute-start.4) | collective-permute-done | bytes 32800 | tf_op jit(solution)/shard_map/ppermute | solution.py:444
  96.6 6.1 %collective-permute-start.5 = (bf16[12,4,512]{2,1,0:T(4,128)(2,1)S(1)}, bf16[12,4,512]{2,1,0:T(4,128)(2,1)S(1)}, u32[]{:S(2)}, u32[]{:S(2)}) collective-permute-start(bf16[12,4,512]{2,1,0:T(4,128)(2,1)S(1)} %get-tuple-element.27), channel_id=1, source_target_pairs={{0,1},{1,2},{2,3},{3,4},{4,5},{5,6},{6,7},{7,8},{8,9},{9,10},{10,1... | collective-permute-start | bytes 147464 | tf_op jit(solution)/shard_map/ppermute | solution.py:442
  102.7 1.9 %collective-permute-start.6 = (bf16[12,4,512]{2,1,0:T(4,128)(2,1)S(1)}, bf16[12,4,512]{2,1,0:T(4,128)(2,1)S(1)}, u32[]{:S(2)}, u32[]{:S(2)}) collective-permute-start(bf16[12,4,512]{2,1,0:T(4,128)(2,1)S(1)} %get-tuple-element.28), channel_id=1, source_target_pairs={{1,0},{2,1},{3,2},{4,3},{5,4},{6,5},{7,6},{8,7},{9,8},{10,9},{11,1... | collective-permute-start | bytes 147464 | tf_op jit(solution)/shard_map/ppermute | solution.py:444
  104.7 1.1 copy-done.2
  105.8 1.1 copy-done.4
  106.9 4.5 %collective-permute-done.6 = bf16[12,4,512]{2,1,0:T(4,128)(2,1)S(1)} collective-permute-done((bf16[12,4,512]{2,1,0:T(4,128)(2,1)S(1)}, bf16[12,4,512]{2,1,0:T(4,128)(2,1)S(1)}, u32[]{:S(2)}, u32[]{:S(2)}) %collective-permute-start.6) | collective-permute-done | bytes 49184 | tf_op jit(solution)/shard_map/ppermute | solution.py:444
  111.4 0.1 pad_maximum_fusion.1.cells_ref
  111.5 2.1 %gru.1 = f32[32,128]{1,0:T(8,128)} custom-call(bf16[12,16,512]{2,1,0:T(8,128)(2,1)S(1)} %pad_maximum_fusion.1.cells_ref, bf16[5,512,256]{2,1,0:T(8,128)(2,1)S(1)} %copy-done, bf16[5,512,128]{2,1,0:T(8,128)(2,1)S(1)} %copy-done.3, bf16[5,512,256]{2,1,0:T(8,128)(2,1)S(1)} %copy-done.1, bf16[5,512,128]{2,1,0:T(8,128)(2,1)S(1)} %copy-done.4, ...), custom_call_target="tpu_custom_call" | custom-call | flops 1000000000 | bytes 5000000 | tf_op jit(solution)/shard_map/gru/pallas_call | solution.py:524
  113.7 0.7 sum_parts.1
  (24 shorter events, 0.1 us)
Async XLA Ops:
  3.0 23.6 %all-to-all-start = ((bf16[8,32,582]{2,1,0:T(8,128)(2,1)}), bf16[8,32,582]{2,1,0:T(8,128)(2,1)S(1)}, u32[]{:S(2)}, u32[]{:S(2)}) async-start(bf16[8,32,582]{2,1,0:T(8,128)(2,1)} %get-tuple-element.15), calls=%async_computation | async-start | bytes 655360 | tf_op jit(solution)/shard_map/all_to_all | solution.py:498
  13.3 24.4 %copy-start.9 = (bf16[384,1024]{1,0:T(8,128)(2,1)S(1)}, bf16[384,1024]{1,0:T(8,128)(2,1)}, u32[]{:S(2)}) copy-start(bf16[384,1024]{1,0:T(8,128)(2,1)} %constant.33.clone.pool_ref) | copy-start | bytes 2359300
  13.3 9.9 %collective-permute-start = (bf16[32,256]{1,0:T(8,128)(2,1)}, bf16[32,256]{1,0:T(8,128)(2,1)S(1)}, u32[]{:S(2)}, u32[]{:S(2)}) collective-permute-start(bf16[32,256]{1,0:T(8,128)(2,1)} %get-tuple-element.16), channel_id=1, source_target_pairs={{0,256},{256,0},{1,257},{257,1},{2,258},{258,2},{3,259},{259,3},{4... | collective-permute-start | bytes 49160 | tf_op jit(solution)/shard_map/ppermute | solution.py:451
  26.6 19.5 %all-to-all-start.1 = ((bf16[16,64,256]{2,1,0:T(8,128)(2,1)}), bf16[16,64,256]{2,1,0:T(8,128)(2,1)S(1)}, u32[]{:S(2)}, u32[]{:S(2)}) async-start(bf16[16,64,256]{2,1,0:T(8,128)(2,1)} %pad_maximum_fusion), calls=%async_computation.1 | async-start | bytes 1048576 | tf_op jit(solution)/shard_map/all_to_all | solution.py:505
  34.2 3.5 %collective-permute-start.1 = (bf16[256,582]{1,0:T(8,128)(2,1)S(1)}, bf16[256,582]{1,0:T(8,128)(2,1)S(1)}, u32[]{:S(2)}, u32[]{:S(2)}) collective-permute-start(bf16[256,582]{1,0:T(8,128)(2,1)S(1)} %bitcast.16), channel_id=1, source_target_pairs={{0,16},{16,0},{1,17},{17,1},{2,18},{18,2},{3,19},{19,3},{4,20},{20... | collective-permute-start | bytes 893960 | tf_op jit(solution)/shard_map/ppermute | solution.py:451
  36.2 9.9 %copy-start.8 = (f32[324,256]{1,0:T(8,128)S(1)}, f32[324,256]{1,0:T(8,128)}, u32[]{:S(2)}) copy-start(f32[324,256]{1,0:T(8,128)} %motion_ref.1) | copy-start | bytes 995332
  45.3 0.8 copy-start.5
  54.3 3.4 %collective-permute-start.2 = (bf16[256,512]{1,0:T(8,128)(2,1)S(1)}, bf16[256,512]{1,0:T(8,128)(2,1)S(1)}, u32[]{:S(2)}, u32[]{:S(2)}) collective-permute-start(bf16[256,512]{1,0:T(8,128)(2,1)S(1)} %get-tuple-element.21), channel_id=1, source_target_pairs={{0,16},{16,0},{1,17},{17,1},{2,18},{18,2},{3,19},{19,3},{4,20},{20... | collective-permute-start | bytes 786440 | tf_op jit(solution)/shard_map/ppermute | solution.py:451
  57.8 25.0 %copy-start.6 = (bf16[4,8,128]{2,1,0:T(8,128)(2,1)S(1)}, bf16[4,8,128]{2,1,0:T(8,128)(2,1)}, u32[]{:S(2)}) copy-start(bf16[4,8,128]{2,1,0:T(8,128)(2,1)} %param.16) | copy-start | bytes 24580
  57.8 25.0 %copy-start.7 = (bf16[4,8,128]{2,1,0:T(8,128)(2,1)S(1)}, bf16[4,8,128]{2,1,0:T(8,128)(2,1)}, u32[]{:S(2)}) copy-start(bf16[4,8,128]{2,1,0:T(8,128)(2,1)} %param.17) | copy-start | bytes 24580
  57.8 46.9 %copy-start.1 = (bf16[5,512,256]{2,1,0:T(8,128)(2,1)S(1)}, bf16[5,512,256]{2,1,0:T(8,128)(2,1)}, u32[]{:S(2)}) copy-start(bf16[5,512,256]{2,1,0:T(8,128)(2,1)} %cg_ref.1) | copy-start | bytes 3932164
  57.8 46.8 %copy-start = (bf16[5,512,256]{2,1,0:T(8,128)(2,1)S(1)}, bf16[5,512,256]{2,1,0:T(8,128)(2,1)}, u32[]{:S(2)}) copy-start(bf16[5,512,256]{2,1,0:T(8,128)(2,1)} %rg_ref.1) | copy-start | bytes 3932164
  75.4 38.2 %all-to-all-start.3 = ((bf16[32,32,256]{2,1,0:T(8,128)(2,1)}), bf16[32,32,256]{2,1,0:T(8,128)(2,1)S(1)}, u32[]{:S(2)}, u32[]{:S(2)}) async-start(bf16[32,32,256]{2,1,0:T(8,128)(2,1)} %copy-done.5), calls=%async_computation.3 | async-start | bytes 1048576 | tf_op jit(solution)/shard_map/all_to_all | solution.py:516
  83.4 11.6 %collective-permute-start.3 = (bf16[4,8,512]{2,1,0:T(8,128)(2,1)S(1)}, bf16[4,8,512]{2,1,0:T(8,128)(2,1)S(1)}, u32[]{:S(2)}, u32[]{:S(2)}) collective-permute-start(bf16[4,8,512]{2,1,0:T(8,128)(2,1)S(1)} %bitcast.19), channel_id=1, source_target_pairs={{0,16},{16,32},{32,48},{48,64},{64,80},{80,96},{96,112},{112,128},... | collective-permute-start | bytes 98312 | tf_op jit(solution)/shard_map/ppermute | solution.py:442
  85.3 11.2 %collective-permute-start.4 = (bf16[4,8,512]{2,1,0:T(8,128)(2,1)S(1)}, bf16[4,8,512]{2,1,0:T(8,128)(2,1)S(1)}, u32[]{:S(2)}, u32[]{:S(2)}) collective-permute-start(bf16[4,8,512]{2,1,0:T(8,128)(2,1)S(1)} %bitcast.20), channel_id=1, source_target_pairs={{16,0},{32,16},{48,32},{64,48},{80,64},{96,80},{112,96},{128,112},... | collective-permute-start | bytes 98312 | tf_op jit(solution)/shard_map/ppermute | solution.py:444
  96.6 10.2 %collective-permute-start.5 = (bf16[12,4,512]{2,1,0:T(4,128)(2,1)S(1)}, bf16[12,4,512]{2,1,0:T(4,128)(2,1)S(1)}, u32[]{:S(2)}, u32[]{:S(2)}) collective-permute-start(bf16[12,4,512]{2,1,0:T(4,128)(2,1)S(1)} %get-tuple-element.27), channel_id=1, source_target_pairs={{0,1},{1,2},{2,3},{3,4},{4,5},{5,6},{6,7},{7,8},{8,9},{9,10},{10,1... | collective-permute-start | bytes 147464 | tf_op jit(solution)/shard_map/ppermute | solution.py:442
  102.7 8.7 %collective-permute-start.6 = (bf16[12,4,512]{2,1,0:T(4,128)(2,1)S(1)}, bf16[12,4,512]{2,1,0:T(4,128)(2,1)S(1)}, u32[]{:S(2)}, u32[]{:S(2)}) collective-permute-start(bf16[12,4,512]{2,1,0:T(4,128)(2,1)S(1)} %get-tuple-element.28), channel_id=1, source_target_pairs={{1,0},{2,1},{3,2},{4,3},{5,4},{6,5},{7,6},{8,7},{9,8},{10,9},{11,1... | collective-permute-start | bytes 147464 | tf_op jit(solution)/shard_map/ppermute | solution.py:444
  104.7 1.1 copy-start.2
  105.8 1.1 copy-start.4
  106.9 4.7 %copy-start.3 = (bf16[5,512,128]{2,1,0:T(8,128)(2,1)S(1)}, bf16[5,512,128]{2,1,0:T(8,128)(2,1)}, u32[]{:S(2)}) copy-start(bf16[5,512,128]{2,1,0:T(8,128)(2,1)} %rc_ref.1) | copy-start | bytes 1966084

commit v4 on v3

--- a/solution.py
+++ b/solution.py
@@ -505,8 +505,8 @@
     right = lax.all_to_all(rights, COL, 0, 0).reshape(targets, channels)
 
     pool = jnp.asarray(pool_matrix(LANES, 2, strip_cols))
-    spread, grad = spread_out(pixels, channels, targets, 32, targets // strip)(place, left_cot, left_cot_other, pool)
-    outgoing, outgoing_other = look_up(pixels, channels, targets, 32)(
+    spread, grad = spread_out(pixels, channels, targets, 128, targets // strip)(place, left_cot, left_cot_other, pool)
+    outgoing, outgoing_other = look_up(pixels, channels, targets, 128)(
         place, left_cot, left_cot_other, right, spread, pool, motion_weight
     )
 

time: 115 us -> 113 us (0.983)
  Pallas kernels: 21.6 us -> 18.1 us
  starting transfers between devices: 53.6 us -> 55.3 us
    pallas_call x2, Pallas kernels: 15.8 us -> 12.3 us  [the longest x1 6.4 us: shards(): look_up(pixels, channels, targets, 128)]
    all_to_all x1, starting transfers between devices: 7.35 us -> 9.05 us  [shards(): grad = lax.all_to_all(grad, SPREAD, 0, 0)]
  transfers between devices with their start and end apart: 10 -> 10, of which waited for: 6 -> 6; matrix products, arithmetic and copies ran while one was open for 2% -> 2% of each run, Pallas kernels for 9% -> 8%
where the time goes in v4:
time: 113 us
  starting transfers between devices  55.3 us (49%)
  Pallas kernels  18.1 us (16%)
  blocking collectives  17.5 us (15%)
  waiting for transfers between devices  15.8 us (14%)
  local copies, waits for them, and re-layouts  3.88 us (3%)
    all_to_all x1, blocking collectives, shards(): parts = lax.all_to_all(outgoing.reshape(zs, cells, 2 * channels), 'z', 0, 0)  17.5 us
    ppermute x2, starting transfers between devices, with_halo(): lax.ppermute(head, axis, [((i + 1) % count, i) for i in range(ends)])  11.6 us
    all_to_all x1, starting transfers between devices, shards(): left_cot = lax.all_to_all(lefts, 'z', 0, 0).reshape(pixels // 2, -1)  10.3 us
    all_to_all x1, starting transfers between devices, shards(): grad = lax.all_to_all(grad, SPREAD, 0, 0)  9.05 us
    ppermute x3, starting transfers between devices, swap(): lax.ppermute(block, axis, [(i, i ^ bit) for i in range(lax.axis_size(axis...  8.78 us
    ppermute x2, starting transfers between devices, with_halo(): lax.ppermute(tail, axis, [(i, (i + 1) % count) for i in range(ends)])  7.98 us
    ppermute x3, waiting for transfers between devices, swap(): lax.ppermute(block, axis, [(i, i ^ bit) for i in range(lax.axis_size(axis...  7.92 us
    all_to_all x1, starting transfers between devices, shards(): right = lax.all_to_all(rights, COL, 0, 0).reshape(targets, channels)  7.57 us
  transfers between devices with their start and end apart: 10, of which 6 were waited for; matrix products, arithmetic and copies ran while one was open for 2% of the time, Pallas kernels for 8%

profile of v4, /device:TPU:56, one launch (start us, length us, event | category | flops | bytes accessed | tf_op | source)
XLA Modules:
  0.0 112.5 jit_solution(9612683135908870709)
XLA Ops:
  0.6 2.4 %pack.1 = (bf16[8,32,582]{2,1,0:T(8,128)(2,1)}, bf16[32,256]{1,0:T(8,128)(2,1)}) custom-call(bf16[32,256]{1,0:T(8,128)(2,1)} %bitcast.28, bf16[32,324]{1,0:T(8,128)(2,1)} %bitcast.26, s32[2,4,128]{2,1,0:T(4,128)} %flow_ref.1, bf16[8,4,256]{2,1,0:T(4,128)(2,1)} %right_ref.1), custom_call_target="tpu_custom_call" | custom-call | tf_op jit(solution)/shard_map/pack/pallas_call | solution.py:491
  3.0 10.3 %all-to-all-start = ((bf16[8,32,582]{2,1,0:T(8,128)(2,1)}), bf16[8,32,582]{2,1,0:T(8,128)(2,1)S(1)}, u32[]{:S(2)}, u32[]{:S(2)}) async-start(bf16[8,32,582]{2,1,0:T(8,128)(2,1)} %get-tuple-element.15), calls=%async_computation | async-start | bytes 655360 | tf_op jit(solution)/shard_map/all_to_all | solution.py:498
  13.3 4.8 %collective-permute-start = (bf16[32,256]{1,0:T(8,128)(2,1)}, bf16[32,256]{1,0:T(8,128)(2,1)S(1)}, u32[]{:S(2)}, u32[]{:S(2)}) collective-permute-start(bf16[32,256]{1,0:T(8,128)(2,1)} %get-tuple-element.16), channel_id=1, source_target_pairs={{0,256},{256,0},{1,257},{257,1},{2,258},{258,2},{3,259},{259,3},{4... | collective-permute-start | bytes 49160 | tf_op jit(solution)/shard_map/ppermute | solution.py:451
  18.2 5.0 %collective-permute-done = bf16[32,256]{1,0:T(8,128)(2,1)S(1)} collective-permute-done((bf16[32,256]{1,0:T(8,128)(2,1)}, bf16[32,256]{1,0:T(8,128)(2,1)S(1)}, u32[]{:S(2)}, u32[]{:S(2)}) %collective-permute-start) | collective-permute-done | bytes 16416 | tf_op jit(solution)/shard_map/ppermute | solution.py:451
  23.2 0.7 broadcast_in_dim.4
  24.0 0.8 pad_maximum_fusion
  24.8 1.8 %all-to-all-done = bf16[8,32,582]{2,1,0:T(8,128)(2,1)S(1)} async-done(((bf16[8,32,582]{2,1,0:T(8,128)(2,1)}), bf16[8,32,582]{2,1,0:T(8,128)(2,1)S(1)}, u32[]{:S(2)}, u32[]{:S(2)}) %all-to-all-start) | async-done | bytes 298016 | tf_op jit(solution)/shard_map/all_to_all | solution.py:498
  26.6 7.6 %all-to-all-start.1 = ((bf16[16,64,256]{2,1,0:T(8,128)(2,1)}), bf16[16,64,256]{2,1,0:T(8,128)(2,1)S(1)}, u32[]{:S(2)}, u32[]{:S(2)}) async-start(bf16[16,64,256]{2,1,0:T(8,128)(2,1)} %pad_maximum_fusion), calls=%async_computation.1 | async-start | bytes 1048576 | tf_op jit(solution)/shard_map/all_to_all | solution.py:505
  34.2 1.9 %collective-permute-start.1 = (bf16[256,582]{1,0:T(8,128)(2,1)S(1)}, bf16[256,582]{1,0:T(8,128)(2,1)S(1)}, u32[]{:S(2)}, u32[]{:S(2)}) collective-permute-start(bf16[256,582]{1,0:T(8,128)(2,1)S(1)} %bitcast.16), channel_id=1, source_target_pairs={{0,16},{16,0},{1,17},{17,1},{2,18},{18,2},{3,19},{19,3},{4,20},{20... | collective-permute-start | bytes 893960 | tf_op jit(solution)/shard_map/ppermute | solution.py:451
  36.1 0.1 stack.23.place
  36.2 1.5 %collective-permute-done.1.other_ref = bf16[256,582]{1,0:T(8,128)(2,1)S(1)} collective-permute-done((bf16[256,582]{1,0:T(8,128)(2,1)S(1)}, bf16[256,582]{1,0:T(8,128)(2,1)S(1)}, u32[]{:S(2)}, u32[]{:S(2)}) %collective-permute-start.1) | collective-permute-done | bytes 298016 | tf_op jit(solution)/shard_map/ppermute | solution.py:451
  37.7 5.9 %spread_out.1 = (bf16[512,1024]{1,0:T(8,128)(2,1)S(1)}, bf16[32,32,256]{2,1,0:T(8,128)(2,1)S(1)}) custom-call(s32[5]{0:T(128)S(1)} %stack.23.place, bf16[256,582]{1,0:T(8,128)(2,1)S(1)} %bitcast.17, bf16[256,582]{1,0:T(8,128)(2,1)S(1)} %collective-permute-done.1.other_ref, bf16[384,1024]{1,0:T(8,128)(2,1)S(1)} %copy-done.9), custom_call_target="tpu_custom_call" | custom-call | flops 5000000000 | bytes 4000000 | tf_op jit(solution)/shard_map/spread_out/pallas_call | solution.py:508
  43.6 0.8 copy-done.5
  44.4 0.0 all-to-all-done.1
  44.4 6.4 %look_up.1 = (f32[256,512]{1,0:T(8,128)S(1)}, bf16[256,512]{1,0:T(8,128)(2,1)S(1)}) custom-call(s32[5]{0:T(128)S(1)} %stack.23.place, bf16[256,582]{1,0:T(8,128)(2,1)S(1)} %bitcast.18, bf16[256,582]{1,0:T(8,128)(2,1)S(1)} %collective-permute-done.1.other_ref, bf16[1024,256]{1,0:T(8,128)(2,1)S(1)} %bitcast.15, ...), custom_call_target="tpu_custom_call" | custom-call | flops 6000000000 | bytes 4000000 | tf_op jit(solution)/shard_map/look_up/pallas_call | solution.py:509
  50.8 2.0 %collective-permute-start.2 = (bf16[256,512]{1,0:T(8,128)(2,1)S(1)}, bf16[256,512]{1,0:T(8,128)(2,1)S(1)}, u32[]{:S(2)}, u32[]{:S(2)}) collective-permute-start(bf16[256,512]{1,0:T(8,128)(2,1)S(1)} %get-tuple-element.21), channel_id=1, source_target_pairs={{0,16},{16,0},{1,17},{17,1},{2,18},{18,2},{3,19},{19,3},{4,20},{20... | collective-permute-start | bytes 786440 | tf_op jit(solution)/shard_map/ppermute | solution.py:451
  52.9 1.4 %collective-permute-done.2 = bf16[256,512]{1,0:T(8,128)(2,1)S(1)} collective-permute-done((bf16[256,512]{1,0:T(8,128)(2,1)S(1)}, bf16[256,512]{1,0:T(8,128)(2,1)S(1)}, u32[]{:S(2)}, u32[]{:S(2)}) %collective-permute-start.2) | collective-permute-done | bytes 262176 | tf_op jit(solution)/shard_map/ppermute | solution.py:451
  54.3 0.1 add_convert_fusion
  54.4 17.5 %all_to_all.20.parts_ref = bf16[8,32,512]{2,1,0:T(8,128)(2,1)S(1)} all-to-all(bf16[8,32,512]{2,1,0:T(8,128)(2,1)S(1)} %bitcast.25), channel_id=1, replica_groups=mesh['yh'=2,'z'=8,'core'=2,'x'=4,'yl'=4] {'z'}, dimensions={0} | all-to-all | bytes 524288 | tf_op jit(solution)/shard_map/all_to_all | solution.py:514
  71.9 9.0 %all-to-all-start.3 = ((bf16[32,32,256]{2,1,0:T(8,128)(2,1)}), bf16[32,32,256]{2,1,0:T(8,128)(2,1)S(1)}, u32[]{:S(2)}, u32[]{:S(2)}) async-start(bf16[32,32,256]{2,1,0:T(8,128)(2,1)} %copy-done.5), calls=%async_computation.3 | async-start | bytes 1048576 | tf_op jit(solution)/shard_map/all_to_all | solution.py:516
  81.0 0.6 add_up.1
  81.6 1.9 %collective-permute-start.3 = (bf16[4,8,512]{2,1,0:T(8,128)(2,1)S(1)}, bf16[4,8,512]{2,1,0:T(8,128)(2,1)S(1)}, u32[]{:S(2)}, u32[]{:S(2)}) collective-permute-start(bf16[4,8,512]{2,1,0:T(8,128)(2,1)S(1)} %bitcast.19), channel_id=1, source_target_pairs={{0,16},{16,32},{32,48},{48,64},{64,80},{80,96},{96,112},{112,128},... | collective-permute-start | bytes 98312 | tf_op jit(solution)/shard_map/ppermute | solution.py:442
  83.5 9.7 %collective-permute-start.4 = (bf16[4,8,512]{2,1,0:T(8,128)(2,1)S(1)}, bf16[4,8,512]{2,1,0:T(8,128)(2,1)S(1)}, u32[]{:S(2)}, u32[]{:S(2)}) collective-permute-start(bf16[4,8,512]{2,1,0:T(8,128)(2,1)S(1)} %bitcast.20), channel_id=1, source_target_pairs={{16,0},{32,16},{48,32},{64,48},{80,64},{96,80},{112,96},{128,112},... | collective-permute-start | bytes 98312 | tf_op jit(solution)/shard_map/ppermute | solution.py:444
  93.2 1.6 %collective-permute-done.4 = bf16[4,8,512]{2,1,0:T(8,128)(2,1)S(1)} collective-permute-done((bf16[4,8,512]{2,1,0:T(8,128)(2,1)S(1)}, bf16[4,8,512]{2,1,0:T(8,128)(2,1)S(1)}, u32[]{:S(2)}, u32[]{:S(2)}) %collective-permute-start.4) | collective-permute-done | bytes 32800 | tf_op jit(solution)/shard_map/ppermute | solution.py:444
  94.8 6.1 %collective-permute-start.5 = (bf16[12,4,512]{2,1,0:T(4,128)(2,1)S(1)}, bf16[12,4,512]{2,1,0:T(4,128)(2,1)S(1)}, u32[]{:S(2)}, u32[]{:S(2)}) collective-permute-start(bf16[12,4,512]{2,1,0:T(4,128)(2,1)S(1)} %get-tuple-element.27), channel_id=1, source_target_pairs={{0,1},{1,2},{2,3},{3,4},{4,5},{5,6},{6,7},{7,8},{8,9},{9,10},{10,1... | collective-permute-start | bytes 147464 | tf_op jit(solution)/shard_map/ppermute | solution.py:442
  100.9 1.9 %collective-permute-start.6 = (bf16[12,4,512]{2,1,0:T(4,128)(2,1)S(1)}, bf16[12,4,512]{2,1,0:T(4,128)(2,1)S(1)}, u32[]{:S(2)}, u32[]{:S(2)}) collective-permute-start(bf16[12,4,512]{2,1,0:T(4,128)(2,1)S(1)} %get-tuple-element.28), channel_id=1, source_target_pairs={{1,0},{2,1},{3,2},{4,3},{5,4},{6,5},{7,6},{8,7},{9,8},{10,9},{11,1... | collective-permute-start | bytes 147464 | tf_op jit(solution)/shard_map/ppermute | solution.py:444
  102.9 1.1 copy-done.2
  103.9 1.1 copy-done.4
  105.0 4.5 %collective-permute-done.6 = bf16[12,4,512]{2,1,0:T(4,128)(2,1)S(1)} collective-permute-done((bf16[12,4,512]{2,1,0:T(4,128)(2,1)S(1)}, bf16[12,4,512]{2,1,0:T(4,128)(2,1)S(1)}, u32[]{:S(2)}, u32[]{:S(2)}) %collective-permute-start.6) | collective-permute-done | bytes 49184 | tf_op jit(solution)/shard_map/ppermute | solution.py:444
  109.6 0.1 pad_maximum_fusion.1.cells_ref
  109.7 2.1 %gru.1 = f32[32,128]{1,0:T(8,128)} custom-call(bf16[12,16,512]{2,1,0:T(8,128)(2,1)S(1)} %pad_maximum_fusion.1.cells_ref, bf16[5,512,256]{2,1,0:T(8,128)(2,1)S(1)} %copy-done, bf16[5,512,128]{2,1,0:T(8,128)(2,1)S(1)} %copy-done.3, bf16[5,512,256]{2,1,0:T(8,128)(2,1)S(1)} %copy-done.1, bf16[5,512,128]{2,1,0:T(8,128)(2,1)S(1)} %copy-done.4, ...), custom_call_target="tpu_custom_call" | custom-call | flops 1000000000 | bytes 5000000 | tf_op jit(solution)/shard_map/gru/pallas_call | solution.py:524
  111.8 0.7 sum_parts.1
  (24 shorter events, 0.1 us)
Async XLA Ops:
  3.0 23.6 %all-to-all-start = ((bf16[8,32,582]{2,1,0:T(8,128)(2,1)}), bf16[8,32,582]{2,1,0:T(8,128)(2,1)S(1)}, u32[]{:S(2)}, u32[]{:S(2)}) async-start(bf16[8,32,582]{2,1,0:T(8,128)(2,1)} %get-tuple-element.15), calls=%async_computation | async-start | bytes 655360 | tf_op jit(solution)/shard_map/all_to_all | solution.py:498
  13.3 24.4 %copy-start.9 = (bf16[384,1024]{1,0:T(8,128)(2,1)S(1)}, bf16[384,1024]{1,0:T(8,128)(2,1)}, u32[]{:S(2)}) copy-start(bf16[384,1024]{1,0:T(8,128)(2,1)} %constant.33.clone.pool_ref) | copy-start | bytes 2359300
  13.3 9.9 %collective-permute-start = (bf16[32,256]{1,0:T(8,128)(2,1)}, bf16[32,256]{1,0:T(8,128)(2,1)S(1)}, u32[]{:S(2)}, u32[]{:S(2)}) collective-permute-start(bf16[32,256]{1,0:T(8,128)(2,1)} %get-tuple-element.16), channel_id=1, source_target_pairs={{0,256},{256,0},{1,257},{257,1},{2,258},{258,2},{3,259},{259,3},{4... | collective-permute-start | bytes 49160 | tf_op jit(solution)/shard_map/ppermute | solution.py:451
  26.6 17.8 %all-to-all-start.1 = ((bf16[16,64,256]{2,1,0:T(8,128)(2,1)}), bf16[16,64,256]{2,1,0:T(8,128)(2,1)S(1)}, u32[]{:S(2)}, u32[]{:S(2)}) async-start(bf16[16,64,256]{2,1,0:T(8,128)(2,1)} %pad_maximum_fusion), calls=%async_computation.1 | async-start | bytes 1048576 | tf_op jit(solution)/shard_map/all_to_all | solution.py:505
  34.2 3.5 %collective-permute-start.1 = (bf16[256,582]{1,0:T(8,128)(2,1)S(1)}, bf16[256,582]{1,0:T(8,128)(2,1)S(1)}, u32[]{:S(2)}, u32[]{:S(2)}) collective-permute-start(bf16[256,582]{1,0:T(8,128)(2,1)S(1)} %bitcast.16), channel_id=1, source_target_pairs={{0,16},{16,0},{1,17},{17,1},{2,18},{18,2},{3,19},{19,3},{4,20},{20... | collective-permute-start | bytes 893960 | tf_op jit(solution)/shard_map/ppermute | solution.py:451
  36.2 8.2 %copy-start.8 = (f32[324,256]{1,0:T(8,128)S(1)}, f32[324,256]{1,0:T(8,128)}, u32[]{:S(2)}) copy-start(f32[324,256]{1,0:T(8,128)} %motion_ref.1) | copy-start | bytes 995332
  43.6 0.8 copy-start.5
  50.8 3.4 %collective-permute-start.2 = (bf16[256,512]{1,0:T(8,128)(2,1)S(1)}, bf16[256,512]{1,0:T(8,128)(2,1)S(1)}, u32[]{:S(2)}, u32[]{:S(2)}) collective-permute-start(bf16[256,512]{1,0:T(8,128)(2,1)S(1)} %get-tuple-element.21), channel_id=1, source_target_pairs={{0,16},{16,0},{1,17},{17,1},{2,18},{18,2},{3,19},{19,3},{4,20},{20... | collective-permute-start | bytes 786440 | tf_op jit(solution)/shard_map/ppermute | solution.py:451
  54.3 26.7 %copy-start.6 = (bf16[4,8,128]{2,1,0:T(8,128)(2,1)S(1)}, bf16[4,8,128]{2,1,0:T(8,128)(2,1)}, u32[]{:S(2)}) copy-start(bf16[4,8,128]{2,1,0:T(8,128)(2,1)} %param.16) | copy-start | bytes 24580
  54.3 26.7 %copy-start.7 = (bf16[4,8,128]{2,1,0:T(8,128)(2,1)S(1)}, bf16[4,8,128]{2,1,0:T(8,128)(2,1)}, u32[]{:S(2)}) copy-start(bf16[4,8,128]{2,1,0:T(8,128)(2,1)} %param.17) | copy-start | bytes 24580
  54.3 48.6 %copy-start.1 = (bf16[5,512,256]{2,1,0:T(8,128)(2,1)S(1)}, bf16[5,512,256]{2,1,0:T(8,128)(2,1)}, u32[]{:S(2)}) copy-start(bf16[5,512,256]{2,1,0:T(8,128)(2,1)} %cg_ref.1) | copy-start | bytes 3932164
  54.4 48.5 %copy-start = (bf16[5,512,256]{2,1,0:T(8,128)(2,1)S(1)}, bf16[5,512,256]{2,1,0:T(8,128)(2,1)}, u32[]{:S(2)}) copy-start(bf16[5,512,256]{2,1,0:T(8,128)(2,1)} %rg_ref.1) | copy-start | bytes 3932164
  71.9 39.9 %all-to-all-start.3 = ((bf16[32,32,256]{2,1,0:T(8,128)(2,1)}), bf16[32,32,256]{2,1,0:T(8,128)(2,1)S(1)}, u32[]{:S(2)}, u32[]{:S(2)}) async-start(bf16[32,32,256]{2,1,0:T(8,128)(2,1)} %copy-done.5), calls=%async_computation.3 | async-start | bytes 1048576 | tf_op jit(solution)/shard_map/all_to_all | solution.py:516
  81.6 11.6 %collective-permute-start.3 = (bf16[4,8,512]{2,1,0:T(8,128)(2,1)S(1)}, bf16[4,8,512]{2,1,0:T(8,128)(2,1)S(1)}, u32[]{:S(2)}, u32[]{:S(2)}) collective-permute-start(bf16[4,8,512]{2,1,0:T(8,128)(2,1)S(1)} %bitcast.19), channel_id=1, source_target_pairs={{0,16},{16,32},{32,48},{48,64},{64,80},{80,96},{96,112},{112,128},... | collective-permute-start | bytes 98312 | tf_op jit(solution)/shard_map/ppermute | solution.py:442
  83.5 11.2 %collective-permute-start.4 = (bf16[4,8,512]{2,1,0:T(8,128)(2,1)S(1)}, bf16[4,8,512]{2,1,0:T(8,128)(2,1)S(1)}, u32[]{:S(2)}, u32[]{:S(2)}) collective-permute-start(bf16[4,8,512]{2,1,0:T(8,128)(2,1)S(1)} %bitcast.20), channel_id=1, source_target_pairs={{16,0},{32,16},{48,32},{64,48},{80,64},{96,80},{112,96},{128,112},... | collective-permute-start | bytes 98312 | tf_op jit(solution)/shard_map/ppermute | solution.py:444
  94.8 10.2 %collective-permute-start.5 = (bf16[12,4,512]{2,1,0:T(4,128)(2,1)S(1)}, bf16[12,4,512]{2,1,0:T(4,128)(2,1)S(1)}, u32[]{:S(2)}, u32[]{:S(2)}) collective-permute-start(bf16[12,4,512]{2,1,0:T(4,128)(2,1)S(1)} %get-tuple-element.27), channel_id=1, source_target_pairs={{0,1},{1,2},{2,3},{3,4},{4,5},{5,6},{6,7},{7,8},{8,9},{9,10},{10,1... | collective-permute-start | bytes 147464 | tf_op jit(solution)/shard_map/ppermute | solution.py:442
  100.9 8.7 %collective-permute-start.6 = (bf16[12,4,512]{2,1,0:T(4,128)(2,1)S(1)}, bf16[12,4,512]{2,1,0:T(4,128)(2,1)S(1)}, u32[]{:S(2)}, u32[]{:S(2)}) collective-permute-start(bf16[12,4,512]{2,1,0:T(4,128)(2,1)S(1)} %get-tuple-element.28), channel_id=1, source_target_pairs={{1,0},{2,1},{3,2},{4,3},{5,4},{6,5},{7,6},{8,7},{9,8},{10,9},{11,1... | collective-permute-start | bytes 147464 | tf_op jit(solution)/shard_map/ppermute | solution.py:444
  102.9 1.1 copy-start.2
  103.9 1.1 copy-start.4
  105.0 4.7 %copy-start.3 = (bf16[5,512,128]{2,1,0:T(8,128)(2,1)S(1)}, bf16[5,512,128]{2,1,0:T(8,128)(2,1)}, u32[]{:S(2)}) copy-start(bf16[5,512,128]{2,1,0:T(8,128)(2,1)} %rc_ref.1) | copy-start | bytes 1966084

commit v5 on v4

--- a/solution.py
+++ b/solution.py
@@ -505,8 +505,8 @@
     right = lax.all_to_all(rights, COL, 0, 0).reshape(targets, channels)
 
     pool = jnp.asarray(pool_matrix(LANES, 2, strip_cols))
-    spread, grad = spread_out(pixels, channels, targets, 128, targets // strip)(place, left_cot, left_cot_other, pool)
-    outgoing, outgoing_other = look_up(pixels, channels, targets, 128)(
+    spread, grad = spread_out(pixels, channels, targets, 256, targets // strip)(place, left_cot, left_cot_other, pool)
+    outgoing, outgoing_other = look_up(pixels, channels, targets, 256)(
         place, left_cot, left_cot_other, right, spread, pool, motion_weight
     )
 

time: 113 us -> 113 us (level)
  transfers between devices with their start and end apart: 10 -> 10, of which waited for: 6 -> 7; matrix products, arithmetic and copies ran while one was open for 2% -> 2% of each run, Pallas kernels for 8% -> 8%
where the time goes in v5:
time: 113 us; the launch traced here: 112 us
  starting transfers between devices  55.2 us (49%)
  Pallas kernels  17.6 us (16%)
  blocking collectives  17.5 us (15%)
  waiting for transfers between devices  16.1 us (14%)
  local copies, waits for them, and re-layouts  3.88 us (3%)
    all_to_all x1, blocking collectives, shards(): parts = lax.all_to_all(outgoing.reshape(zs, cells, 2 * channels), 'z', 0, 0)  17.5 us
    ppermute x2, starting transfers between devices, with_halo(): lax.ppermute(head, axis, [((i + 1) % count, i) for i in range(ends)])  11.6 us
    all_to_all x1, starting transfers between devices, shards(): left_cot = lax.all_to_all(lefts, 'z', 0, 0).reshape(pixels // 2, -1)  10.3 us
    all_to_all x1, starting transfers between devices, shards(): grad = lax.all_to_all(grad, SPREAD, 0, 0)  9.11 us
    ppermute x3, starting transfers between devices, swap(): lax.ppermute(block, axis, [(i, i ^ bit) for i in range(lax.axis_size(axis...  8.67 us
    ppermute x3, waiting for transfers between devices, swap(): lax.ppermute(block, axis, [(i, i ^ bit) for i in range(lax.axis_size(axis...  8.03 us
    ppermute x2, starting transfers between devices, with_halo(): lax.ppermute(tail, axis, [(i, (i + 1) % count) for i in range(ends)])  7.98 us
    all_to_all x1, starting transfers between devices, shards(): right = lax.all_to_all(rights, COL, 0, 0).reshape(targets, channels)  7.57 us
  transfers between devices with their start and end apart: 10, of which 7 were waited for; matrix products, arithmetic and copies ran while one was open for 2% of the time, Pallas kernels for 8%

profile of v5, /device:TPU:56, one launch (start us, length us, event | category | flops | bytes accessed | tf_op | source)
XLA Modules:
  0.0 112.2 jit_solution(5603527641408599266)
XLA Ops:
  0.6 2.4 %pack.1 = (bf16[8,32,582]{2,1,0:T(8,128)(2,1)}, bf16[32,256]{1,0:T(8,128)(2,1)}) custom-call(bf16[32,256]{1,0:T(8,128)(2,1)} %bitcast.28, bf16[32,324]{1,0:T(8,128)(2,1)} %bitcast.26, s32[2,4,128]{2,1,0:T(4,128)} %flow_ref.1, bf16[8,4,256]{2,1,0:T(4,128)(2,1)} %right_ref.1), custom_call_target="tpu_custom_call" | custom-call | tf_op jit(solution)/shard_map/pack/pallas_call | solution.py:491
  3.0 10.3 %all-to-all-start = ((bf16[8,32,582]{2,1,0:T(8,128)(2,1)}), bf16[8,32,582]{2,1,0:T(8,128)(2,1)S(1)}, u32[]{:S(2)}, u32[]{:S(2)}) async-start(bf16[8,32,582]{2,1,0:T(8,128)(2,1)} %get-tuple-element.15), calls=%async_computation | async-start | bytes 655360 | tf_op jit(solution)/shard_map/all_to_all | solution.py:498
  13.3 4.8 %collective-permute-start = (bf16[32,256]{1,0:T(8,128)(2,1)}, bf16[32,256]{1,0:T(8,128)(2,1)S(1)}, u32[]{:S(2)}, u32[]{:S(2)}) collective-permute-start(bf16[32,256]{1,0:T(8,128)(2,1)} %get-tuple-element.16), channel_id=1, source_target_pairs={{0,256},{256,0},{1,257},{257,1},{2,258},{258,2},{3,259},{259,3},{4... | collective-permute-start | bytes 49160 | tf_op jit(solution)/shard_map/ppermute | solution.py:451
  18.2 5.0 %collective-permute-done = bf16[32,256]{1,0:T(8,128)(2,1)S(1)} collective-permute-done((bf16[32,256]{1,0:T(8,128)(2,1)}, bf16[32,256]{1,0:T(8,128)(2,1)S(1)}, u32[]{:S(2)}, u32[]{:S(2)}) %collective-permute-start) | collective-permute-done | bytes 16416 | tf_op jit(solution)/shard_map/ppermute | solution.py:451
  23.2 0.7 broadcast_in_dim.4
  24.0 0.8 pad_maximum_fusion
  24.8 1.8 %all-to-all-done = bf16[8,32,582]{2,1,0:T(8,128)(2,1)S(1)} async-done(((bf16[8,32,582]{2,1,0:T(8,128)(2,1)}), bf16[8,32,582]{2,1,0:T(8,128)(2,1)S(1)}, u32[]{:S(2)}, u32[]{:S(2)}) %all-to-all-start) | async-done | bytes 298016 | tf_op jit(solution)/shard_map/all_to_all | solution.py:498
  26.6 7.6 %all-to-all-start.1 = ((bf16[16,64,256]{2,1,0:T(8,128)(2,1)}), bf16[16,64,256]{2,1,0:T(8,128)(2,1)S(1)}, u32[]{:S(2)}, u32[]{:S(2)}) async-start(bf16[16,64,256]{2,1,0:T(8,128)(2,1)} %pad_maximum_fusion), calls=%async_computation.1 | async-start | bytes 1048576 | tf_op jit(solution)/shard_map/all_to_all | solution.py:505
  34.2 1.9 %collective-permute-start.1 = (bf16[256,582]{1,0:T(8,128)(2,1)S(1)}, bf16[256,582]{1,0:T(8,128)(2,1)S(1)}, u32[]{:S(2)}, u32[]{:S(2)}) collective-permute-start(bf16[256,582]{1,0:T(8,128)(2,1)S(1)} %bitcast.16), channel_id=1, source_target_pairs={{0,16},{16,0},{1,17},{17,1},{2,18},{18,2},{3,19},{19,3},{4,20},{20... | collective-permute-start | bytes 893960 | tf_op jit(solution)/shard_map/ppermute | solution.py:451
  36.1 0.1 stack.23.place
  36.2 1.5 %collective-permute-done.1.other_ref = bf16[256,582]{1,0:T(8,128)(2,1)S(1)} collective-permute-done((bf16[256,582]{1,0:T(8,128)(2,1)S(1)}, bf16[256,582]{1,0:T(8,128)(2,1)S(1)}, u32[]{:S(2)}, u32[]{:S(2)}) %collective-permute-start.1) | collective-permute-done | bytes 298016 | tf_op jit(solution)/shard_map/ppermute | solution.py:451
  37.7 5.7 %spread_out.1 = (bf16[512,1024]{1,0:T(8,128)(2,1)S(1)}, bf16[32,32,256]{2,1,0:T(8,128)(2,1)S(1)}) custom-call(s32[5]{0:T(128)S(1)} %stack.23.place, bf16[256,582]{1,0:T(8,128)(2,1)S(1)} %bitcast.17, bf16[256,582]{1,0:T(8,128)(2,1)S(1)} %collective-permute-done.1.other_ref, bf16[384,1024]{1,0:T(8,128)(2,1)S(1)} %copy-done.9), custom_call_target="tpu_custom_call" | custom-call | flops 5000000000 | bytes 4000000 | tf_op jit(solution)/shard_map/spread_out/pallas_call | solution.py:508
  43.4 0.8 copy-done.5
  44.2 0.2 all-to-all-done.1
  44.4 6.1 %look_up.1 = (f32[256,512]{1,0:T(8,128)S(1)}, bf16[256,512]{1,0:T(8,128)(2,1)S(1)}) custom-call(s32[5]{0:T(128)S(1)} %stack.23.place, bf16[256,582]{1,0:T(8,128)(2,1)S(1)} %bitcast.18, bf16[256,582]{1,0:T(8,128)(2,1)S(1)} %collective-permute-done.1.other_ref, bf16[1024,256]{1,0:T(8,128)(2,1)S(1)} %bitcast.15, ...), custom_call_target="tpu_custom_call" | custom-call | flops 6000000000 | bytes 4000000 | tf_op jit(solution)/shard_map/look_up/pallas_call | solution.py:509
  50.5 1.9 %collective-permute-start.2 = (bf16[256,512]{1,0:T(8,128)(2,1)S(1)}, bf16[256,512]{1,0:T(8,128)(2,1)S(1)}, u32[]{:S(2)}, u32[]{:S(2)}) collective-permute-start(bf16[256,512]{1,0:T(8,128)(2,1)S(1)} %get-tuple-element.21), channel_id=1, source_target_pairs={{0,16},{16,0},{1,17},{17,1},{2,18},{18,2},{3,19},{19,3},{4,20},{20... | collective-permute-start | bytes 786440 | tf_op jit(solution)/shard_map/ppermute | solution.py:451
  52.4 1.5 %collective-permute-done.2 = bf16[256,512]{1,0:T(8,128)(2,1)S(1)} collective-permute-done((bf16[256,512]{1,0:T(8,128)(2,1)S(1)}, bf16[256,512]{1,0:T(8,128)(2,1)S(1)}, u32[]{:S(2)}, u32[]{:S(2)}) %collective-permute-start.2) | collective-permute-done | bytes 262176 | tf_op jit(solution)/shard_map/ppermute | solution.py:451
  53.9 0.1 add_convert_fusion
  54.0 17.5 %all_to_all.20.parts_ref = bf16[8,32,512]{2,1,0:T(8,128)(2,1)S(1)} all-to-all(bf16[8,32,512]{2,1,0:T(8,128)(2,1)S(1)} %bitcast.25), channel_id=1, replica_groups=mesh['yh'=2,'z'=8,'core'=2,'x'=4,'yl'=4] {'z'}, dimensions={0} | all-to-all | bytes 524288 | tf_op jit(solution)/shard_map/all_to_all | solution.py:514
  71.5 9.1 %all-to-all-start.3 = ((bf16[32,32,256]{2,1,0:T(8,128)(2,1)}), bf16[32,32,256]{2,1,0:T(8,128)(2,1)S(1)}, u32[]{:S(2)}, u32[]{:S(2)}) async-start(bf16[32,32,256]{2,1,0:T(8,128)(2,1)} %copy-done.5), calls=%async_computation.3 | async-start | bytes 1048576 | tf_op jit(solution)/shard_map/all_to_all | solution.py:516
  80.6 0.6 add_up.1
  81.3 1.9 %collective-permute-start.3 = (bf16[4,8,512]{2,1,0:T(8,128)(2,1)S(1)}, bf16[4,8,512]{2,1,0:T(8,128)(2,1)S(1)}, u32[]{:S(2)}, u32[]{:S(2)}) collective-permute-start(bf16[4,8,512]{2,1,0:T(8,128)(2,1)S(1)} %bitcast.19), channel_id=1, source_target_pairs={{0,16},{16,32},{32,48},{48,64},{64,80},{80,96},{96,112},{112,128},... | collective-permute-start | bytes 98312 | tf_op jit(solution)/shard_map/ppermute | solution.py:442
  83.2 9.7 %collective-permute-start.4 = (bf16[4,8,512]{2,1,0:T(8,128)(2,1)S(1)}, bf16[4,8,512]{2,1,0:T(8,128)(2,1)S(1)}, u32[]{:S(2)}, u32[]{:S(2)}) collective-permute-start(bf16[4,8,512]{2,1,0:T(8,128)(2,1)S(1)} %bitcast.20), channel_id=1, source_target_pairs={{16,0},{32,16},{48,32},{64,48},{80,64},{96,80},{112,96},{128,112},... | collective-permute-start | bytes 98312 | tf_op jit(solution)/shard_map/ppermute | solution.py:444
  92.9 1.6 %collective-permute-done.4 = bf16[4,8,512]{2,1,0:T(8,128)(2,1)S(1)} collective-permute-done((bf16[4,8,512]{2,1,0:T(8,128)(2,1)S(1)}, bf16[4,8,512]{2,1,0:T(8,128)(2,1)S(1)}, u32[]{:S(2)}, u32[]{:S(2)}) %collective-permute-start.4) | collective-permute-done | bytes 32800 | tf_op jit(solution)/shard_map/ppermute | solution.py:444
  94.5 6.1 %collective-permute-start.5 = (bf16[12,4,512]{2,1,0:T(4,128)(2,1)S(1)}, bf16[12,4,512]{2,1,0:T(4,128)(2,1)S(1)}, u32[]{:S(2)}, u32[]{:S(2)}) collective-permute-start(bf16[12,4,512]{2,1,0:T(4,128)(2,1)S(1)} %get-tuple-element.27), channel_id=1, source_target_pairs={{0,1},{1,2},{2,3},{3,4},{4,5},{5,6},{6,7},{7,8},{8,9},{9,10},{10,1... | collective-permute-start | bytes 147464 | tf_op jit(solution)/shard_map/ppermute | solution.py:442
  100.6 1.9 %collective-permute-start.6 = (bf16[12,4,512]{2,1,0:T(4,128)(2,1)S(1)}, bf16[12,4,512]{2,1,0:T(4,128)(2,1)S(1)}, u32[]{:S(2)}, u32[]{:S(2)}) collective-permute-start(bf16[12,4,512]{2,1,0:T(4,128)(2,1)S(1)} %get-tuple-element.28), channel_id=1, source_target_pairs={{1,0},{2,1},{3,2},{4,3},{5,4},{6,5},{7,6},{8,7},{9,8},{10,9},{11,1... | collective-permute-start | bytes 147464 | tf_op jit(solution)/shard_map/ppermute | solution.py:444
  102.5 1.1 copy-done.2
  103.6 1.1 copy-done.4
  104.7 4.5 %collective-permute-done.6 = bf16[12,4,512]{2,1,0:T(4,128)(2,1)S(1)} collective-permute-done((bf16[12,4,512]{2,1,0:T(4,128)(2,1)S(1)}, bf16[12,4,512]{2,1,0:T(4,128)(2,1)S(1)}, u32[]{:S(2)}, u32[]{:S(2)}) %collective-permute-start.6) | collective-permute-done | bytes 49184 | tf_op jit(solution)/shard_map/ppermute | solution.py:444
  109.2 0.1 pad_maximum_fusion.1.cells_ref
  109.4 2.1 %gru.1 = f32[32,128]{1,0:T(8,128)} custom-call(bf16[12,16,512]{2,1,0:T(8,128)(2,1)S(1)} %pad_maximum_fusion.1.cells_ref, bf16[5,512,256]{2,1,0:T(8,128)(2,1)S(1)} %copy-done, bf16[5,512,128]{2,1,0:T(8,128)(2,1)S(1)} %copy-done.3, bf16[5,512,256]{2,1,0:T(8,128)(2,1)S(1)} %copy-done.1, bf16[5,512,128]{2,1,0:T(8,128)(2,1)S(1)} %copy-done.4, ...), custom_call_target="tpu_custom_call" | custom-call | flops 1000000000 | bytes 5000000 | tf_op jit(solution)/shard_map/gru/pallas_call | solution.py:524
  111.5 0.7 sum_parts.1
  (24 shorter events, 0.1 us)
Async XLA Ops:
  3.0 23.6 %all-to-all-start = ((bf16[8,32,582]{2,1,0:T(8,128)(2,1)}), bf16[8,32,582]{2,1,0:T(8,128)(2,1)S(1)}, u32[]{:S(2)}, u32[]{:S(2)}) async-start(bf16[8,32,582]{2,1,0:T(8,128)(2,1)} %get-tuple-element.15), calls=%async_computation | async-start | bytes 655360 | tf_op jit(solution)/shard_map/all_to_all | solution.py:498
  13.3 24.4 %copy-start.9 = (bf16[384,1024]{1,0:T(8,128)(2,1)S(1)}, bf16[384,1024]{1,0:T(8,128)(2,1)}, u32[]{:S(2)}) copy-start(bf16[384,1024]{1,0:T(8,128)(2,1)} %constant.33.clone.pool_ref) | copy-start | bytes 2359300
  13.3 9.9 %collective-permute-start = (bf16[32,256]{1,0:T(8,128)(2,1)}, bf16[32,256]{1,0:T(8,128)(2,1)S(1)}, u32[]{:S(2)}, u32[]{:S(2)}) collective-permute-start(bf16[32,256]{1,0:T(8,128)(2,1)} %get-tuple-element.16), channel_id=1, source_target_pairs={{0,256},{256,0},{1,257},{257,1},{2,258},{258,2},{3,259},{259,3},{4... | collective-permute-start | bytes 49160 | tf_op jit(solution)/shard_map/ppermute | solution.py:451
  26.6 17.8 %all-to-all-start.1 = ((bf16[16,64,256]{2,1,0:T(8,128)(2,1)}), bf16[16,64,256]{2,1,0:T(8,128)(2,1)S(1)}, u32[]{:S(2)}, u32[]{:S(2)}) async-start(bf16[16,64,256]{2,1,0:T(8,128)(2,1)} %pad_maximum_fusion), calls=%async_computation.1 | async-start | bytes 1048576 | tf_op jit(solution)/shard_map/all_to_all | solution.py:505
  34.2 3.5 %collective-permute-start.1 = (bf16[256,582]{1,0:T(8,128)(2,1)S(1)}, bf16[256,582]{1,0:T(8,128)(2,1)S(1)}, u32[]{:S(2)}, u32[]{:S(2)}) collective-permute-start(bf16[256,582]{1,0:T(8,128)(2,1)S(1)} %bitcast.16), channel_id=1, source_target_pairs={{0,16},{16,0},{1,17},{17,1},{2,18},{18,2},{3,19},{19,3},{4,20},{20... | collective-permute-start | bytes 893960 | tf_op jit(solution)/shard_map/ppermute | solution.py:451
  36.2 8.2 %copy-start.8 = (f32[324,256]{1,0:T(8,128)S(1)}, f32[324,256]{1,0:T(8,128)}, u32[]{:S(2)}) copy-start(f32[324,256]{1,0:T(8,128)} %motion_ref.1) | copy-start | bytes 995332
  43.4 0.8 copy-start.5
  50.5 3.4 %collective-permute-start.2 = (bf16[256,512]{1,0:T(8,128)(2,1)S(1)}, bf16[256,512]{1,0:T(8,128)(2,1)S(1)}, u32[]{:S(2)}, u32[]{:S(2)}) collective-permute-start(bf16[256,512]{1,0:T(8,128)(2,1)S(1)} %get-tuple-element.21), channel_id=1, source_target_pairs={{0,16},{16,0},{1,17},{17,1},{2,18},{18,2},{3,19},{19,3},{4,20},{20... | collective-permute-start | bytes 786440 | tf_op jit(solution)/shard_map/ppermute | solution.py:451
  53.9 26.7 %copy-start.6 = (bf16[4,8,128]{2,1,0:T(8,128)(2,1)S(1)}, bf16[4,8,128]{2,1,0:T(8,128)(2,1)}, u32[]{:S(2)}) copy-start(bf16[4,8,128]{2,1,0:T(8,128)(2,1)} %param.16) | copy-start | bytes 24580
  53.9 26.7 %copy-start.7 = (bf16[4,8,128]{2,1,0:T(8,128)(2,1)S(1)}, bf16[4,8,128]{2,1,0:T(8,128)(2,1)}, u32[]{:S(2)}) copy-start(bf16[4,8,128]{2,1,0:T(8,128)(2,1)} %param.17) | copy-start | bytes 24580
  53.9 48.6 %copy-start.1 = (bf16[5,512,256]{2,1,0:T(8,128)(2,1)S(1)}, bf16[5,512,256]{2,1,0:T(8,128)(2,1)}, u32[]{:S(2)}) copy-start(bf16[5,512,256]{2,1,0:T(8,128)(2,1)} %cg_ref.1) | copy-start | bytes 3932164
  54.0 48.5 %copy-start = (bf16[5,512,256]{2,1,0:T(8,128)(2,1)S(1)}, bf16[5,512,256]{2,1,0:T(8,128)(2,1)}, u32[]{:S(2)}) copy-start(bf16[5,512,256]{2,1,0:T(8,128)(2,1)} %rg_ref.1) | copy-start | bytes 3932164
  71.5 40.0 %all-to-all-start.3 = ((bf16[32,32,256]{2,1,0:T(8,128)(2,1)}), bf16[32,32,256]{2,1,0:T(8,128)(2,1)S(1)}, u32[]{:S(2)}, u32[]{:S(2)}) async-start(bf16[32,32,256]{2,1,0:T(8,128)(2,1)} %copy-done.5), calls=%async_computation.3 | async-start | bytes 1048576 | tf_op jit(solution)/shard_map/all_to_all | solution.py:516
  81.3 11.6 %collective-permute-start.3 = (bf16[4,8,512]{2,1,0:T(8,128)(2,1)S(1)}, bf16[4,8,512]{2,1,0:T(8,128)(2,1)S(1)}, u32[]{:S(2)}, u32[]{:S(2)}) collective-permute-start(bf16[4,8,512]{2,1,0:T(8,128)(2,1)S(1)} %bitcast.19), channel_id=1, source_target_pairs={{0,16},{16,32},{32,48},{48,64},{64,80},{80,96},{96,112},{112,128},... | collective-permute-start | bytes 98312 | tf_op jit(solution)/shard_map/ppermute | solution.py:442
  83.2 11.2 %collective-permute-start.4 = (bf16[4,8,512]{2,1,0:T(8,128)(2,1)S(1)}, bf16[4,8,512]{2,1,0:T(8,128)(2,1)S(1)}, u32[]{:S(2)}, u32[]{:S(2)}) collective-permute-start(bf16[4,8,512]{2,1,0:T(8,128)(2,1)S(1)} %bitcast.20), channel_id=1, source_target_pairs={{16,0},{32,16},{48,32},{64,48},{80,64},{96,80},{112,96},{128,112},... | collective-permute-start | bytes 98312 | tf_op jit(solution)/shard_map/ppermute | solution.py:444
  94.5 10.2 %collective-permute-start.5 = (bf16[12,4,512]{2,1,0:T(4,128)(2,1)S(1)}, bf16[12,4,512]{2,1,0:T(4,128)(2,1)S(1)}, u32[]{:S(2)}, u32[]{:S(2)}) collective-permute-start(bf16[12,4,512]{2,1,0:T(4,128)(2,1)S(1)} %get-tuple-element.27), channel_id=1, source_target_pairs={{0,1},{1,2},{2,3},{3,4},{4,5},{5,6},{6,7},{7,8},{8,9},{9,10},{10,1... | collective-permute-start | bytes 147464 | tf_op jit(solution)/shard_map/ppermute | solution.py:442
  100.6 8.7 %collective-permute-start.6 = (bf16[12,4,512]{2,1,0:T(4,128)(2,1)S(1)}, bf16[12,4,512]{2,1,0:T(4,128)(2,1)S(1)}, u32[]{:S(2)}, u32[]{:S(2)}) collective-permute-start(bf16[12,4,512]{2,1,0:T(4,128)(2,1)S(1)} %get-tuple-element.28), channel_id=1, source_target_pairs={{1,0},{2,1},{3,2},{4,3},{5,4},{6,5},{7,6},{8,7},{9,8},{10,9},{11,1... | collective-permute-start | bytes 147464 | tf_op jit(solution)/shard_map/ppermute | solution.py:444
  102.5 1.1 copy-start.2
  103.6 1.1 copy-start.4
  104.7 4.7 %copy-start.3 = (bf16[5,512,128]{2,1,0:T(8,128)(2,1)S(1)}, bf16[5,512,128]{2,1,0:T(8,128)(2,1)}, u32[]{:S(2)}) copy-start(bf16[5,512,128]{2,1,0:T(8,128)(2,1)} %rc_ref.1) | copy-start | bytes 1966084
